TPU v7x, 32 devices: a whole 2x2x4 slice. The times are simulated.
32 devices in a mesh: pb: 4 (over y, core), ka: 8 (over z, x).
Axes of the slice: x: 2, y: 2, z: 4, core: 2. Of those that a mesh axis runs over, the one named last changes fastest.
Arguments:
- teacher_q: float32 [2, 3072, 256], P(None, 'ka')
- student_q: float32 [2, 3072, 128], P(None, 'ka')
Outputs:
- query_grad: float32 [2, 3072, 128], P(None, 'ka')
- loss: float32 [], replicated
All inputs are finite; a program needn't handle non-finite values.
Results may differ from a plain program's by a relative error of at most 0.00029.
Values sent between devices are 32-bit elements; how exact they have to be, the bound alone decides.
A program may use at most 64 MiB of HBM per device.

v0:
```python
import math

import jax
import jax.numpy as jnp
from jax import lax
from jax.sharding import PartitionSpec as P

HEADS = 1
DT = 256
DS = 128


precise = lax.Precision.HIGHEST


def from_root(x, axis, root):
    mine = lax.axis_index(axis) == root
    return lax.psum(jnp.where(mine, x, jnp.zeros_like(x)), axis)


def fetch_block(teacher_q, student_q):
    share_count = lax.axis_size("ka") // lax.axis_size("pb")
    leading = lax.axis_index("pb") * share_count
    teacher_parts = []
    student_parts = []
    for offset in range(share_count):
        teacher_piece, student_piece = (
            from_root(teacher_q, "ka", leading + offset),
            from_root(student_q, "ka", leading + offset),
        )
        teacher_parts.append(teacher_piece)
        student_parts.append(student_piece)
    return (jnp.concatenate(teacher_parts, axis=1), jnp.concatenate(student_parts, axis=1))


def relation_tiles(teacher_rows, student_rows, teacher_columns, student_columns):
    batches = teacher_rows.shape[0]
    row_count = teacher_rows.shape[1]
    column_count = teacher_columns.shape[1]
    teacher_tile = jnp.einsum(
        "brhd,bchd->bhrc",
        teacher_rows.reshape(batches, row_count, HEADS, DT),
        teacher_columns.reshape(batches, column_count, HEADS, DT),
        precision=precise,
        preferred_element_type=jnp.float32,
    ) * (1.0 / math.sqrt(DT))
    student_tile = jnp.einsum(
        "brhd,bchd->bhrc",
        student_rows.reshape(batches, row_count, HEADS, DS),
        student_columns.reshape(batches, column_count, HEADS, DS),
        precision=precise,
        preferred_element_type=jnp.float32,
    ) * (1.0 / math.sqrt(DS))
    return (teacher_tile, student_tile)


def exponentials(teacher_tile, student_tile, teacher_max, student_max):
    teacher_exp = jnp.exp(teacher_tile - teacher_max[..., None])
    student_exp = jnp.exp(student_tile - student_max[..., None])
    local_sums = (
        jnp.sum(teacher_exp, axis=3),
        jnp.sum(teacher_exp * (teacher_tile - student_tile), axis=3),
        jnp.sum(student_exp, axis=3),
    )
    return (teacher_exp, student_exp, local_sums)


def statistics_ka(teacher_tile, student_tile):
    teacher_max, student_max = lax.pmax(
        (jnp.max(teacher_tile, axis=3), jnp.max(student_tile, axis=3)), "ka"
    )
    teacher_exp, student_exp, local_sums = exponentials(
        teacher_tile, student_tile, teacher_max, student_max
    )
    teacher_sum, cross, student_sum = lax.psum((local_sums[0], local_sums[1], local_sums[2]), "ka")
    return (teacher_max, student_max, teacher_exp, student_exp, teacher_sum, cross, student_sum)


def gradients(statistics):
    teacher_max, student_max, teacher_exp, student_exp, teacher_sum, cross, student_sum = statistics
    divergence = (
        cross / teacher_sum
        - teacher_max
        - jnp.log(teacher_sum)
        + student_max
        + jnp.log(student_sum)
    )
    grad_tile = (
        student_exp / student_sum[..., None] - teacher_exp / teacher_sum[..., None]
    ) / HEADS
    return (divergence, grad_tile)


def rows_product(grad_tile, column_student):
    batches = column_student.shape[0]
    column_count = column_student.shape[1]
    product = jnp.einsum(
        "bhrc,bchd->brhd",
        grad_tile,
        column_student.reshape(batches, column_count, HEADS, DS),
        precision=precise,
        preferred_element_type=jnp.float32,
    )
    return product.reshape(batches, grad_tile.shape[2], HEADS * DS) * (1.0 / math.sqrt(DS))


def columns_product(grad_tile, row_student):
    batches = row_student.shape[0]
    row_count = row_student.shape[1]
    product = jnp.einsum(
        "bhrc,brhd->bchd",
        grad_tile,
        row_student.reshape(batches, row_count, HEADS, DS),
        precision=precise,
        preferred_element_type=jnp.float32,
    )
    return product.reshape(batches, grad_tile.shape[3], HEADS * DS) * (1.0 / math.sqrt(DS))


def own_total(values):
    return lax.psum(values, "pb")


def block_total(values):
    return lax.psum(values, "ka")


def own_share(block_grad, own_rows):
    share_count = lax.axis_size("ka") // lax.axis_size("pb")
    column_index = lax.axis_index("ka")
    piece = lax.dynamic_slice_in_dim(block_grad, column_index % share_count * own_rows, own_rows, 1)
    return from_root(piece, "pb", column_index // share_count)


def shards(teacher_q, student_q):
    batches = teacher_q.shape[0]
    own_rows = teacher_q.shape[1]
    teacher_block, student_block = fetch_block(teacher_q, student_q)
    teacher_tile, student_tile = relation_tiles(teacher_block, student_block, teacher_q, student_q)
    divergence, grad_tile = gradients(statistics_ka(teacher_tile, student_tile))
    block_grad = block_total(rows_product(grad_tile, student_q))
    own_grad = own_total(columns_product(grad_tile, student_block))
    summed = lax.psum(jnp.sum(divergence), "pb")
    total_rows = teacher_block.shape[1] * lax.axis_size("pb")
    query_grad = own_grad + own_share(block_grad, own_rows)
    loss = summed / (batches * HEADS * total_rows)
    return (query_grad, loss)


def solution(mesh):
    in_specs = (P(None, "ka", None), P(None, "ka", None))
    out_specs = (P(None, "ka", None), P())
    return jax.shard_map(shards, mesh=mesh, in_specs=in_specs, out_specs=out_specs, check_vma=False)
```

profile of v0, /device:TPU:0, one launch (start us, length us, event | category | flops | bytes accessed | tf_op | source)
XLA Modules:
  0.0 333.7 jit_solution(3908216136147039863)
XLA Ops:
  7.2 0.0 all-reduce.11.cloned.1.call-start
  7.2 1.9 broadcast_select_fusion.2
  9.1 2.4 broadcast_select_fusion.1
  11.6 0.0 copy-start.1
  11.6 0.0 all-reduce.11.cloned.1.call-update
  11.6 0.0 all-reduce.7.cloned.1.call-start
  11.6 113.4 %all-reduce.11.cloned.1.call-done = (f32[2,384,128]{2,1,0:T(8,128)}, f32[2,384,128]{2,1,0:T(8,128)}, f32[2,384,256]{2,1,0:T(8,128)}, f32[2,384,256]{2,1,0:T(8,128)}) async-done(((f32[2,384,128]{2,1,0:T(8,128)}, f32[2,384,128]{2,1,0:T(8,128)}, f32[2,384,256]{2,1,0:T(8,128)}, f32[2,384,256]{2,1,0:T(8,128)}), (f32[2,384,128]{2,1,0:T(8,128)}, f32[2,384,128]{2,1,0:T(8,128)}, f32[2,384,256]{2,1,0:T(8,128)}, ...) | async-done | bytes 2359312 | tf_op jit(solution)/shard_map/psum | solution.py:18
  125.0 1.0 constant_dynamic-update-slice_fusion.1
  126.0 0.0 copy-start.2
  126.1 0.0 copy-start.3
  126.1 0.0 copy-start.4
  126.1 1.2 constant_dynamic-update-slice_fusion
  127.3 0.0 copy-done.1
  127.3 4.1 %multiply_reduce_fusion.2 = (f32[2,768]{1,0:T(2,128)}, f32[2,768,384]{1,2,0:T(8,128)}) fusion(f32[2,768,128]{2,1,0:T(8,128)S(1)} %constant_dynamic-update-slice_fusion, f32[2,384,128]{2,1,0:T(8,128)S(1)} %copy-done.1), kind=kOutput, calls=%fused_computation.7 | convolution fusion | flops 907147776 | bytes 3545088 | tf_op jit(solution)/shard_map/brhd,bchd->bhrc/dot_general | solution.py:47
  131.3 0.0 copy-done.2
  131.3 0.0 copy-done.3
  131.3 0.0 copy-done.4
  131.3 2.8 multiply_reduce_fusion.1
  134.2 35.1 %all-reduce.2 = (f32[2,1,768]{2,0,1:T(2,128)S(1)}, f32[2,1,768]{2,0,1:T(2,128)S(1)}) all-reduce(f32[2,1,768]{2,0,1:T(2,128)} %bitcast.28, f32[2,1,768]{2,0,1:T(2,128)} %bitcast.34), channel_id=1, replica_groups=mesh['pb'=4,'ka'=8] {'ka'}, use_global_device_ids=true, to_apply=%region_9.10 | all-reduce | flops 3072 | bytes 24576 | tf_op jit(solution)/shard_map/pmax | solution.py:69
  169.3 3.3 multiply_reduce_fusion
  172.6 34.2 %all-reduce = (f32[2,1,768]{2,0,1:T(2,128)}, f32[2,1,768]{2,0,1:T(2,128)}, f32[2,1,768]{2,0,1:T(2,128)}) all-reduce(f32[2,1,768]{2,0,1:T(2,128)} %bitcast.30, f32[2,1,768]{2,0,1:T(2,128)} %bitcast.31, f32[2,1,768]{2,0,1:T(2,128)} %bitcast.29), channel_id=1, replica_groups=mesh['pb'=4,'ka'=8] {'ka'}, use_global_device_ids=true, to_apply=%region_11.12 | all-reduce | flops 4608 | bytes 36864 | tf_op jit(solution)/shard_map/psum | solution.py:75
  206.7 2.5 divide_subtract_fusion
  209.2 0.0 copy-start
  209.3 1.4 copy-done
  210.7 5.0 %convolution_multiply_fusion = f32[2,768,128]{2,1,0:T(8,128)} fusion(f32[2,768,384]{1,2,0:T(8,128)S(1)} %divide_subtract_fusion, f32[2,384,128]{2,1,0:T(8,128)S(1)} %copy-done.1), kind=kOutput, calls=%fused_computation.12 | convolution fusion | flops 906166272 | bytes 3538944 | tf_op jit(solution)/shard_map/bhrc,bchd->brhd/dot_general | solution.py:97
  215.6 0.0 all-reduce.7.cloned.1.call-update
  215.6 0.0 copy-start.5
  215.7 0.0 copy-start.6
  215.7 0.0 copy-start.7
  215.7 0.2 all-reduce.9.cloned.1.call-start
  215.9 71.8 %all-reduce.7.cloned.1.call-done = f32[2,768,128]{2,1,0:T(8,128)} async-done(((f32[2,768,128]{2,1,0:T(8,128)}), f32[2,768,128]{2,1,0:T(8,128)}) %all-reduce.7.cloned.1.call-update) | async-done | bytes 786448 | tf_op jit(solution)/shard_map/psum | solution.py:125
  287.8 4.5 %fusion.7 = f32[2,384,128]{2,1,0:T(8,128)} fusion(f32[2,768,128]{2,1,0:T(8,128)S(1)} %constant_dynamic-update-slice_fusion, f32[2,768,384]{1,2,0:T(8,128)} %copy-done, f32[2,768,128]{2,1,0:T(8,128)} %all-reduce.7.cloned.1.call-done, s32[]{:T(128)S(6)} %select_n.59, pred[]{:T(512)S(6)} %eq.15), kind=kOutput, calls=%fused_computation.15 | convolution fusion | flops 906264576 | bytes 3932165 | tf_op jit(solution)/shard_map/bhrc,brhd->bchd/dot_general | solution.py:110
  292.3 0.0 all-reduce.9.cloned.1.call-update
  292.3 0.0 copy-done.5
  292.3 0.0 copy-done.6
  292.4 0.0 copy-done.7
  292.4 0.6 add_reduce_fusion
  293.0 6.3 %psum.87 = f32[]{:T(128)} all-reduce(f32[]{:T(128)} %add_reduce_fusion), channel_id=1, replica_groups=mesh['pb'=4,'ka'=8] {'pb'}, use_global_device_ids=true, to_apply=%region_18.19 | all-reduce | flops 1 | bytes 8 | tf_op jit(solution)/shard_map/psum | solution.py:143
  299.9 24.3 %all-reduce.9.cloned.1.call-done = f32[2,384,128]{2,1,0:T(8,128)} async-done(((f32[2,384,128]{2,1,0:T(8,128)}), f32[2,384,128]{2,1,0:T(8,128)}) %all-reduce.9.cloned.1.call-update) | async-done | bytes 393232 | tf_op jit(solution)/shard_map/psum | solution.py:121
  324.2 1.8 copy.19
Async XLA Ops:
  7.2 117.9 %all-reduce.11.cloned.1.call-start = ((), (), s32[]{:S(2)}) async-start(), calls=%async_computation.2 | async-start | bytes 4718592 | tf_op jit(solution)/shard_map/psum | solution.py:18
  11.6 115.7 %copy-start.1 = (f32[2,384,128]{2,1,0:T(8,128)S(1)}, f32[2,384,128]{2,1,0:T(8,128)}, u32[]{:S(2)}) copy-start(f32[2,384,128]{2,1,0:T(8,128)} %param.3) | copy-start | bytes 1179652
  11.6 276.2 %all-reduce.7.cloned.1.call-start = ((), (), s32[]{:S(2)}) async-start(), calls=%async_computation | async-start | bytes 1572864 | tf_op jit(solution)/shard_map/psum | solution.py:125
  126.0 5.3 %copy-start.2 = (f32[2,384,256]{2,1,0:T(8,128)S(1)}, f32[2,384,256]{2,1,0:T(8,128)}, u32[]{:S(2)}) copy-start(f32[2,384,256]{2,1,0:T(8,128)} %param.2) | copy-start | bytes 2359300
  126.1 5.3 %copy-start.3 = (f32[2,384,256]{2,1,0:T(8,128)S(1)}, f32[2,384,256]{2,1,0:T(8,128)}, u32[]{:S(2)}) copy-start(f32[2,384,256]{2,1,0:T(8,128)} %get-tuple-element.10) | copy-start | bytes 2359300
  126.1 5.3 %copy-start.4 = (f32[2,384,256]{2,1,0:T(8,128)S(1)}, f32[2,384,256]{2,1,0:T(8,128)}, u32[]{:S(2)}) copy-start(f32[2,384,256]{2,1,0:T(8,128)} %get-tuple-element.11) | copy-start | bytes 2359300
  209.2 1.4 copy-start
  215.6 76.7 %copy-start.5 = (f32[2,1,768]{2,0,1:T(2,128)S(1)}, f32[2,1,768]{2,0,1:T(2,128)}, u32[]{:S(2)}) copy-start(f32[2,1,768]{2,0,1:T(2,128)} %get-tuple-element.5) | copy-start | bytes 18436
  215.7 76.7 %copy-start.6 = (f32[2,1,768]{2,0,1:T(2,128)S(1)}, f32[2,1,768]{2,0,1:T(2,128)}, u32[]{:S(2)}) copy-start(f32[2,1,768]{2,0,1:T(2,128)} %get-tuple-element.6) | copy-start | bytes 18436
  215.7 76.7 %copy-start.7 = (f32[2,1,768]{2,0,1:T(2,128)S(1)}, f32[2,1,768]{2,0,1:T(2,128)}, u32[]{:S(2)}) copy-start(f32[2,1,768]{2,0,1:T(2,128)} %get-tuple-element.7) | copy-start | bytes 18436
  215.7 108.6 %all-reduce.9.cloned.1.call-start = ((), (), s32[]{:S(2)}) async-start(), calls=%async_computation.1 | async-start | bytes 786432 | tf_op jit(solution)/shard_map/psum | solution.py:121
Sparse Core Ops, SparseCore 0:
  12.4 112.5 all-reduce.10
  215.8 71.9 all-reduce.6
  292.5 31.7 all-reduce.8
where the time goes:
time: 334 us
  waiting for transfers between devices  210 us (63%)
  blocking collectives  75.5 us (23%)
  matrix products  16.4 us (5%)
  between operations  15.7 us (5%)
  other arithmetic  10.8 us (3%)
  local copies, waits for them, and re-layouts  5.4 us (2%)
    psum x1, waiting for transfers between devices, from_root(): return lax.psum(jnp.where(mine, x, jnp.zeros_like(x)), axis)  113 us
    psum x1, waiting for transfers between devices, block_total(): return lax.psum(values, 'ka')  71.8 us
    pmax x1, blocking collectives, statistics_ka(): lax.pmax((jnp.max(teacher_tile, axis=3), jnp.max(student_tile, axis=3)),...  35.1 us
    psum x1, blocking collectives, statistics_ka(): lax.psum((local_sums[0], local_sums[1], local_sums[2]), 'ka')  34.2 us
    psum x1, waiting for transfers between devices, own_total(): return lax.psum(values, 'pb')  24.3 us
  transfers between devices with their start and end apart: 3, of which 3 were waited for; matrix products, arithmetic and copies ran while one was open for 0% of the time, Pallas kernels for 0%

commit v1 on v0

v1 whole, which is shorter than its diff:
```python
import functools
import math

import jax
import jax.numpy as jnp
from jax import lax
from jax.experimental import pallas as pl
from jax.experimental.pallas import tpu as pltpu
from jax.sharding import PartitionSpec as P

HEADS = 1
DT = 256
DS = 128
CHUNK = 64
MESH = pl.DeviceIdType.MESH
LOG2E = 1.4426950408889634
LN2 = 0.6931471805599453


def split(values):
    high = values.astype(jnp.bfloat16)
    low = (values - high.astype(jnp.float32)).astype(jnp.bfloat16)
    return high, low


def nt(left, right):
    return lax.dot_general(
        left, right, (((1,), (1,)), ((), ())), preferred_element_type=jnp.float32
    )


def nn(left, right):
    return jnp.dot(left, right, preferred_element_type=jnp.float32)


def kernel(
    groups, levels, rows, batches,
    t_hbm, s_hbm, out_ref, loss_ref,
    own_t, own_s, nbr_t, nbr_s, col_t, col_s, row_t, row_s, t_sc, s_sc, acc,
    stat_in, level_in, wide, q_tr, w_high, w_low, part, part_in, total_in,
    load_sem, slot_sem, x_send, x_recv, z_send, z_recv,
    stat_send, stat_recv, level_send, level_recv, part_send, part_recv,
    out_send, out_recv,
):
    chunks = rows // CHUNK
    pb = lax.axis_index("pb")
    ka = lax.axis_index("ka")
    seq = pb % batches
    y = pb // batches
    z = ka // 2
    x = ka % 2
    place = x * groups + y
    low = jnp.where(seq == 0, y, groups - 1 - y)
    high = levels - 1 - low
    sources = (low, high)
    mate = y * batches + (1 - seq)
    x_device = (pb, z * 2 + (1 - x))

    planes = []
    for step in range(1, 2 * groups):
        other = (place + step) % (2 * groups)
        planes.append(((other % groups) * batches + seq, z * 2 + other // groups))
    line = [(pb, ((z + step) % levels) * 2 + x) for step in range(1, levels)]
    everyone = planes + line + [(mate, ka)]
    barrier = pltpu.get_barrier_semaphore()
    for device in everyone:
        pl.semaphore_signal(barrier, inc=1, device_id=device, device_id_type=MESH)

    loads = [
        pltpu.make_async_copy(t_hbm.at[seq], own_t, load_sem.at[0]),
        pltpu.make_async_copy(s_hbm.at[seq], own_s, load_sem.at[1]),
    ]
    for slot in range(2):
        @pl.when(z == sources[slot])
        def _():
            pltpu.make_async_copy(t_hbm.at[seq], col_t.at[slot], slot_sem.at[slot, 0]).start()
            pltpu.make_async_copy(s_hbm.at[seq], col_s.at[slot], slot_sem.at[slot, 1]).start()
    for load in loads:
        load.start()
    pl.semaphore_wait(barrier, len(everyone))

    x_copies = [
        pltpu.make_async_remote_copy(
            src_ref=src.at[seq], dst_ref=dst, send_sem=x_send.at[i], recv_sem=x_recv.at[i],
            device_id=x_device, device_id_type=MESH,
        )
        for i, (src, dst) in enumerate(((t_hbm, nbr_t), (s_hbm, nbr_s)))
    ]

    def z_copies(slot, j, way):
        step = 1 if way == 0 else -1
        span = pl.ds(pl.multiple_of(j * CHUNK, CHUNK), CHUNK)
        return [
            pltpu.make_async_remote_copy(
                src_ref=buf.at[slot, span, :], dst_ref=buf.at[slot, span, :],
                send_sem=z_send.at[way, slot, j, i], recv_sem=z_recv.at[slot, j, i],
                device_id=(pb, (z + step) * 2 + x), device_id_type=MESH,
            )
            for i, buf in enumerate((col_t, col_s))
        ]

    for slot in range(2):
        @pl.when(z == sources[slot])
        def _():
            pltpu.make_async_copy(t_hbm.at[seq], col_t.at[slot], slot_sem.at[slot, 0]).wait()
            pltpu.make_async_copy(s_hbm.at[seq], col_s.at[slot], slot_sem.at[slot, 1]).wait()

    def going(slot):
        up = jnp.logical_and(z >= sources[slot], z < levels - 1)
        down = jnp.logical_and(z <= sources[slot], z > 0)
        return ((0, up), (1, down))

    def put_rows(xb, teacher, student):
        t_high, t_low = split(teacher * (LOG2E / math.sqrt(DT)))
        s_high, s_low = split(student * (LOG2E / math.sqrt(DS)))
        row_t[xb] = jnp.concatenate([t_high, t_low, t_high], axis=1)
        row_s[xb] = jnp.concatenate([s_high, s_low, s_high], axis=1)

    def fold(values, how):
        return how(values.reshape(CHUNK // 8, 8, rows), axis=0)

    def relate(xb, slot, j):
        span = pl.ds(pl.multiple_of(j * CHUNK, CHUNK), CHUNK)
        t_high, t_low = split(col_t[slot, span, :])
        s_high, s_low = split(col_s[slot, span, :])
        teacher = nt(jnp.concatenate([t_high, t_high, t_low], axis=1), row_t[xb])
        student = nt(jnp.concatenate([s_high, s_high, s_low], axis=1), row_s[xb])
        at = pl.ds(pl.multiple_of(slot * rows + j * CHUNK, CHUNK), CHUNK)
        t_sc[xb, at, :] = teacher
        s_sc[xb, at, :] = student
        t_old, s_old = acc[xb, 0], acc[xb, 3]
        t_max = jnp.maximum(t_old, fold(teacher, jnp.max))
        s_max = jnp.maximum(s_old, fold(student, jnp.max))
        t_scale = jnp.exp2(t_old - t_max)
        s_scale = jnp.exp2(s_old - s_max)
        t_three = teacher.reshape(CHUNK // 8, 8, rows)
        s_three = student.reshape(CHUNK // 8, 8, rows)
        t_exp = jnp.exp2(t_three - t_max[None])
        s_exp = jnp.exp2(s_three - s_max[None])
        acc[xb, 0] = t_max
        acc[xb, 1] = acc[xb, 1] * t_scale + jnp.sum(t_exp, axis=0)
        acc[xb, 2] = acc[xb, 2] * t_scale + jnp.sum(t_exp * (t_three - s_three), axis=0)
        acc[xb, 3] = s_max
        acc[xb, 4] = acc[xb, 4] * s_scale + jnp.sum(s_exp, axis=0)

    for xb in range(2):
        for kind in range(5):
            start = -jnp.inf if kind in (0, 3) else 0.0
            acc[xb, kind] = jnp.full((8, rows), start, jnp.float32)

    def first_send():
        for slot in range(2):
            for way, goes in going(slot):
                @pl.when(jnp.logical_and(goes, z == sources[slot]))
                def _():
                    def send(j, carry):
                        for copy in z_copies(slot, j, way):
                            copy.start()
                        return carry
                    lax.fori_loop(0, chunks, send, 0)

    first_send()
    for copy in x_copies:
        copy.start()
    for load in loads:
        load.wait()
    put_rows(x, own_t[...], own_s[...])

    def gather(j, carry):
        for slot in range(2):
            @pl.when(z != sources[slot])
            def _():
                for copy in z_copies(slot, j, 0):
                    copy.wait_recv()
                for way, goes in going(slot):
                    @pl.when(goes)
                    def _():
                        for copy in z_copies(slot, j, way):
                            copy.start()
        for slot in range(2):
            relate(x, slot, j)
        return carry

    lax.fori_loop(0, chunks, gather, 0)
    for copy in x_copies:
        copy.wait_recv()
    put_rows(1 - x, nbr_t[...], nbr_s[...])

    def second(j, carry):
        for slot in range(2):
            relate(1 - x, slot, j)
        return carry

    lax.fori_loop(0, chunks, second, 0)

    for xb in range(2):
        t_max, s_max = acc[xb, 0], acc[xb, 3]
        t_top = jnp.max(t_max, axis=0, keepdims=True)
        s_top = jnp.max(s_max, axis=0, keepdims=True)
        t_scale = jnp.exp2(t_max - t_top)
        s_scale = jnp.exp2(s_max - s_top)
        t_sum = jnp.sum(acc[xb, 1] * t_scale, axis=0, keepdims=True)
        cross = jnp.sum(acc[xb, 2] * t_scale, axis=0, keepdims=True)
        s_sum = jnp.sum(acc[xb, 4] * s_scale, axis=0, keepdims=True)
        stat_in[place, xb] = jnp.concatenate(
            [t_top, t_sum, cross, s_top, s_sum, jnp.zeros((3, rows), jnp.float32)], axis=0
        )

    def stat_copy(step):
        return pltpu.make_async_remote_copy(
            src_ref=stat_in.at[place], dst_ref=stat_in.at[place],
            send_sem=stat_send.at[step], recv_sem=stat_recv.at[step],
            device_id=planes[step - 1], device_id_type=MESH,
        )

    def stat_wait(step):
        return pltpu.make_async_remote_copy(
            src_ref=stat_in.at[(place - step + 2 * groups) % (2 * groups)],
            dst_ref=stat_in.at[(place - step + 2 * groups) % (2 * groups)],
            send_sem=stat_send.at[step], recv_sem=stat_recv.at[step],
            device_id=planes[step - 1], device_id_type=MESH,
        )

    for step in range(1, 2 * groups):
        stat_copy(step).start()
    for slot in range(2):
        high_part, low_part = split((col_s[slot] * (1.0 / math.sqrt(DS))).T)
        q_tr[0:DS, slot * rows:(slot + 1) * rows] = high_part
        q_tr[DS:2 * DS, slot * rows:(slot + 1) * rows] = low_part
    for step in range(1, 2 * groups):
        stat_wait(step).wait_recv()

    t_max = stat_in[0, :, 0:1, :]
    s_max = stat_in[0, :, 3:4, :]
    for other in range(1, 2 * groups):
        t_max = jnp.maximum(t_max, stat_in[other, :, 0:1, :])
        s_max = jnp.maximum(s_max, stat_in[other, :, 3:4, :])
    t_sum = cross = s_sum = jnp.zeros((2, 1, rows), jnp.float32)
    for other in range(2 * groups):
        t_scale = jnp.exp2(stat_in[other, :, 0:1, :] - t_max)
        s_scale = jnp.exp2(stat_in[other, :, 3:4, :] - s_max)
        t_sum = t_sum + stat_in[other, :, 1:2, :] * t_scale
        cross = cross + stat_in[other, :, 2:3, :] * t_scale
        s_sum = s_sum + stat_in[other, :, 4:5, :] * s_scale
    t_level = t_max + jnp.log2(t_sum)
    s_level = s_max + jnp.log2(s_sum)
    divergence = LN2 * (cross / t_sum - t_level + s_level)
    both = jnp.broadcast_to(jnp.sum(divergence, axis=0), (6, rows))
    wide[...] = jnp.concatenate([t_level, s_level], axis=1)
    level_in[z] = jnp.concatenate([wide[x], both], axis=0)

    def level_copy(step, slot):
        return pltpu.make_async_remote_copy(
            src_ref=level_in.at[slot], dst_ref=level_in.at[slot],
            send_sem=level_send.at[step], recv_sem=level_recv.at[step],
            device_id=line[step - 1], device_id_type=MESH,
        )

    for step in range(1, levels):
        level_copy(step, z).start()
    for step in range(1, levels):
        level_copy(step, (z - step + levels) % levels).wait_recv()
    columns = [level_in[source].T for source in sources]

    def part_copy(step):
        other = (place + step) % (2 * groups)
        return pltpu.make_async_remote_copy(
            src_ref=part.at[other // groups], dst_ref=part_in.at[step],
            send_sem=part_send.at[step], recv_sem=part_recv.at[step],
            device_id=planes[step - 1], device_id_type=MESH,
        )

    def gradient(xb):
        rows_t = wide[xb, 0:1, :]
        rows_s = wide[xb, 1:2, :]
        for slot in range(2):
            for j in range(chunks):
                at = slice(slot * rows + j * CHUNK, slot * rows + (j + 1) * CHUNK)
                col = columns[slot][j * CHUNK:(j + 1) * CHUNK]
                teacher = t_sc[xb, at, :]
                student = s_sc[xb, at, :]
                weight = (
                    jnp.exp2(student - rows_s) + jnp.exp2(student - col[:, 1:2])
                    - jnp.exp2(teacher - rows_t) - jnp.exp2(teacher - col[:, 0:1])
                )
                high_part, low_part = split(weight)
                w_high[at, :] = high_part
                w_low[at, :] = low_part
        first = nn(q_tr[...], w_high[...])
        part[xb] = first[:DS] + first[DS:] + nn(q_tr[0:DS, :], w_low[...])

    gradient(1 - x)
    for step in range(1, 2 * groups):
        other = (place + step) % (2 * groups)
        @pl.when(other // groups != x)
        def _():
            part_copy(step).start()
    gradient(x)
    for step in range(1, 2 * groups):
        other = (place + step) % (2 * groups)
        @pl.when(other // groups == x)
        def _():
            part_copy(step).start()
    total = level_in[0, 2:3, :]
    for level in range(1, levels):
        total = total + level_in[level, 2:3, :]
    total_in[seq] = jnp.broadcast_to(total, (8, rows))
    total_copy = pltpu.make_async_remote_copy(
        src_ref=total_in.at[seq], dst_ref=total_in.at[seq],
        send_sem=out_send.at[1], recv_sem=out_recv.at[1],
        device_id=(mate, ka), device_id_type=MESH,
    )
    total_copy.start()
    result = part[x]
    for step in range(1, 2 * groups):
        part_copy(step).wait_recv()
        result = result + part_in[step]
    out_ref[seq] = result.T
    out_copy = pltpu.make_async_remote_copy(
        src_ref=out_ref.at[seq], dst_ref=out_ref.at[seq],
        send_sem=out_send.at[0], recv_sem=out_recv.at[0],
        device_id=(mate, ka), device_id_type=MESH,
    )
    out_copy.start()
    total_copy.wait_send()
    pltpu.make_async_remote_copy(
        src_ref=total_in.at[1 - seq], dst_ref=total_in.at[1 - seq],
        send_sem=out_send.at[1], recv_sem=out_recv.at[1],
        device_id=(mate, ka), device_id_type=MESH,
    ).wait_recv()
    loss_ref[0, 0] = jnp.sum(total_in[0, 0:1, :] + total_in[1, 0:1, :]) / (
        batches * HEADS * rows * 2 * levels
    )
    for copy in x_copies:
        copy.wait_send()
    for slot in range(2):
        for way, goes in going(slot):
            @pl.when(goes)
            def _():
                def done(j, carry):
                    for copy in z_copies(slot, j, way):
                        copy.wait_send()
                    return carry
                lax.fori_loop(0, chunks, done, 0)
    for step in range(1, 2 * groups):
        stat_copy(step).wait_send()
        part_copy(step).wait_send()
    for step in range(1, levels):
        level_copy(step, z).wait_send()
    out_copy.wait_send()
    pltpu.make_async_remote_copy(
        src_ref=out_ref.at[1 - seq], dst_ref=out_ref.at[1 - seq],
        send_sem=out_send.at[0], recv_sem=out_recv.at[0],
        device_id=(mate, ka), device_id_type=MESH,
    ).wait_recv()


def solution(mesh):
    def shards(teacher_q, student_q):
        batches, rows = teacher_q.shape[0], teacher_q.shape[1]
        groups = mesh.shape["pb"] // batches
        levels = mesh.shape["ka"] // 2
        chunks = rows // CHUNK
        f32, bf16 = jnp.float32, jnp.bfloat16
        dma = pltpu.SemaphoreType.DMA
        grad, loss = pl.pallas_call(
            functools.partial(kernel, groups, levels, rows, batches),
            out_shape=(
                jax.ShapeDtypeStruct((batches, rows, DS), f32),
                jax.ShapeDtypeStruct((1, 1), f32),
            ),
            in_specs=[pl.BlockSpec(memory_space=pl.ANY)] * 2,
            out_specs=(
                pl.BlockSpec(memory_space=pltpu.VMEM),
                pl.BlockSpec(memory_space=pltpu.SMEM),
            ),
            scratch_shapes=[
                pltpu.VMEM((rows, DT), f32),
                pltpu.VMEM((rows, DS), f32),
                pltpu.VMEM((rows, DT), f32),
                pltpu.VMEM((rows, DS), f32),
                pltpu.VMEM((2, rows, DT), f32),
                pltpu.VMEM((2, rows, DS), f32),
                pltpu.VMEM((2, rows, 3 * DT), bf16),
                pltpu.VMEM((2, rows, 3 * DS), bf16),
                pltpu.VMEM((2, 2 * rows, rows), f32),
                pltpu.VMEM((2, 2 * rows, rows), f32),
                pltpu.VMEM((2, 5, 8, rows), f32),
                pltpu.VMEM((2 * groups, 2, 8, rows), f32),
                pltpu.VMEM((levels, 8, rows), f32),
                pltpu.VMEM((2, 2, rows), f32),
                pltpu.VMEM((2 * DS, 2 * rows), bf16),
                pltpu.VMEM((2 * rows, rows), bf16),
                pltpu.VMEM((2 * rows, rows), bf16),
                pltpu.VMEM((2, DS, rows), f32),
                pltpu.VMEM((2 * groups, DS, rows), f32),
                pltpu.VMEM((batches, 8, rows), f32),
                dma((2,)),
                dma((2, 2)),
                dma((2,)),
                dma((2,)),
                dma((2, 2, chunks, 2)),
                dma((2, chunks, 2)),
                dma((2 * groups,)),
                dma((2 * groups,)),
                dma((levels,)),
                dma((levels,)),
                dma((2 * groups,)),
                dma((2 * groups,)),
                dma((2,)),
                dma((2,)),
            ],
            compiler_params=pltpu.CompilerParams(
                collective_id=0, has_side_effects=True, vmem_limit_bytes=48 * 1024 * 1024
            ),
        )(teacher_q, student_q)
        return grad, loss.reshape(())

    in_specs = (P(None, "ka", None), P(None, "ka", None))
    out_specs = (P(None, "ka", None), P())
    return jax.shard_map(shards, mesh=mesh, in_specs=in_specs, out_specs=out_specs, check_vma=False)
```

time: 334 us -> 87 us (0.26)
  waiting for transfers between devices: 210 us -> 0 us
  Pallas kernels: 0 us -> 81.5 us
  blocking collectives: 75.5 us -> 0 us
  matrix products: 16.4 us -> 0 us
  between operations: 15.7 us -> 2.41 us
  other arithmetic: 10.8 us -> 0 us
    psum x3 -> x0, waiting for transfers between devices: 210 us -> none  [the longest x1 113 us: from_root(): return lax.psum(jnp.where(mine, x, jnp.zeros_like(x)), axis)]
    pallas_call x0 -> x1, Pallas kernels: none -> 81.5 us  [shards(): pl.pallas_call(functools.partial(kernel, groups, levels, rows, batches),...]
    psum x2 -> x0, blocking collectives: 40.4 us -> none  [the longest x1 34.2 us: statistics_ka(): lax.psum((local_sums[0], local_sums[1], local_sums[2]), 'ka')]
    pmax x1 -> x0, blocking collectives: 35.1 us -> none  [statistics_ka(): lax.pmax((jnp.max(teacher_tile, axis=3), jnp.max(student_tile, axis=3)),...]
    dot_general x4 -> x0, matrix products: 16.4 us -> none  [the longest x1 4.96 us: rows_product(): jnp.einsum('bhrc,bchd->brhd', grad_tile, column_student.reshape(batches,...]
    select_n x2 -> x0, other arithmetic: 4.34 us -> none  [from_root(): return lax.psum(jnp.where(mine, x, jnp.zeros_like(x)), axis)]
    reduce_sum x2 -> x0, other arithmetic: 3.91 us -> none  [the longest x1 3.29 us: exponentials(): jnp.sum(teacher_exp * (teacher_tile - student_tile), axis=3)]
  transfers between devices with their start and end apart: 3 -> 0, of which waited for: 3 -> 0; matrix products, arithmetic and copies ran while one was open for 0% -> 0% of each run, Pallas kernels for 0% -> 0%
where the time goes in v1:
time: 87 us; the launch traced here: 86.7 us
  Pallas kernels  81.5 us (94%)
  local copies, waits for them, and re-layouts  2.87 us (3%)
  between operations  2.41 us (3%)
    pallas_call x1, Pallas kernels, shards(): pl.pallas_call(functools.partial(kernel, groups, levels, rows, batches),...  81.5 us
    unnamed x5, local copies, waits for them, and re-layouts  2.87 us

profile of v1, /device:TPU:0, one launch (start us, length us, event | category | flops | bytes accessed | tf_op | source)
XLA Modules:
  0.0 86.7 jit_solution(5550277127760298741)
XLA Ops:
  0.6 0.0 copy-start
  0.6 1.1 %copy-done = f32[2,384,256]{2,1,0:T(8,128)S(1)} copy-done((f32[2,384,256]{2,1,0:T(8,128)S(1)}, f32[2,384,256]{2,1,0:T(8,128)}, u32[]{:S(2)}) %copy-start) | copy-done | bytes 786456
  1.8 0.0 copy-start.1
  1.8 1.0 %copy-done.1 = f32[2,384,128]{2,1,0:T(8,128)S(1)} copy-done((f32[2,384,128]{2,1,0:T(8,128)S(1)}, f32[2,384,128]{2,1,0:T(8,128)}, u32[]{:S(2)}) %copy-start.1) | copy-done | bytes 393240
  2.8 81.5 %shard_map.41 = (f32[2,384,128]{2,1,0:T(8,128)S(1)}, f32[1,1]{1,0:T(1,128)}) custom-call(f32[2,384,256]{2,1,0:T(8,128)S(1)} %copy-done, f32[2,384,128]{2,1,0:T(8,128)S(1)} %copy-done.1), custom_call_target="tpu_custom_call" | custom-call | tf_op jit(solution)/shard_map/pallas_call | solution.py:366
  84.2 0.7 copy.6
Async XLA Ops:
  0.6 1.1 %copy-start = (f32[2,384,256]{2,1,0:T(8,128)S(1)}, f32[2,384,256]{2,1,0:T(8,128)}, u32[]{:S(2)}) copy-start(f32[2,384,256]{2,1,0:T(8,128)} %t_hbm.1) | copy-start | bytes 2359300
  1.8 1.0 %copy-start.1 = (f32[2,384,128]{2,1,0:T(8,128)S(1)}, f32[2,384,128]{2,1,0:T(8,128)}, u32[]{:S(2)}) copy-start(f32[2,384,128]{2,1,0:T(8,128)} %s_hbm.1) | copy-start | bytes 1179652

commit v2 on v1

--- a/solution.py
+++ b/solution.py
@@ -11,7 +11,8 @@
 HEADS = 1
 DT = 256
 DS = 128
-CHUNK = 64
+CHUNK = 96
+TILE = 64
 MESH = pl.DeviceIdType.MESH
 LOG2E = 1.4426950408889634
 LN2 = 0.6931471805599453
@@ -37,7 +38,7 @@
     groups, levels, rows, batches,
     t_hbm, s_hbm, out_ref, loss_ref,
     own_t, own_s, nbr_t, nbr_s, col_t, col_s, row_t, row_s, t_sc, s_sc, acc,
-    stat_in, level_in, wide, q_tr, w_high, w_low, part, part_in, total_in,
+    stat_in, level_in, wide, col_level, w_row, q_tr, w_high, w_low, part, part_in, total_in,
     load_sem, slot_sem, x_send, x_recv, z_send, z_recv,
     stat_send, stat_recv, level_send, level_recv, part_send, part_recv,
     out_send, out_recv,
@@ -87,14 +88,13 @@
         for i, (src, dst) in enumerate(((t_hbm, nbr_t), (s_hbm, nbr_s)))
     ]
 
-    def z_copies(slot, j, way):
-        step = 1 if way == 0 else -1
+    def z_copies(slot, j, to):
         span = pl.ds(pl.multiple_of(j * CHUNK, CHUNK), CHUNK)
         return [
             pltpu.make_async_remote_copy(
                 src_ref=buf.at[slot, span, :], dst_ref=buf.at[slot, span, :],
-                send_sem=z_send.at[way, slot, j, i], recv_sem=z_recv.at[slot, j, i],
-                device_id=(pb, (z + step) * 2 + x), device_id_type=MESH,
+                send_sem=z_send.at[to, slot, j, i], recv_sem=z_recv.at[slot, j, i],
+                device_id=(pb, to * 2 + x), device_id_type=MESH,
             )
             for i, buf in enumerate((col_t, col_s))
         ]
@@ -105,10 +105,17 @@
             pltpu.make_async_copy(t_hbm.at[seq], col_t.at[slot], slot_sem.at[slot, 0]).wait()
             pltpu.make_async_copy(s_hbm.at[seq], col_s.at[slot], slot_sem.at[slot, 1]).wait()
 
-    def going(slot):
-        up = jnp.logical_and(z >= sources[slot], z < levels - 1)
-        down = jnp.logical_and(z <= sources[slot], z > 0)
-        return ((0, up), (1, down))
+    last = levels - 1
+
+    def source_sends(slot, to):
+        near = abs(z - to) == 1
+        reach = (to != z) if 0 < to < last else near
+        return jnp.logical_and(z == sources[slot], reach)
+
+    def forwards(slot, to):
+        beside = 1 if to == 0 else last - 1
+        waits = jnp.logical_and(sources[slot] != z, sources[slot] != to)
+        return jnp.logical_and(z == beside, waits)
 
     def put_rows(xb, teacher, student):
         t_high, t_low = split(teacher * (LOG2E / math.sqrt(DT)))
@@ -116,25 +123,23 @@
         row_t[xb] = jnp.concatenate([t_high, t_low, t_high], axis=1)
         row_s[xb] = jnp.concatenate([s_high, s_low, s_high], axis=1)
 
-    def fold(values, how):
-        return how(values.reshape(CHUNK // 8, 8, rows), axis=0)
-
-    def relate(xb, slot, j):
+    def relate(xb, j):
         span = pl.ds(pl.multiple_of(j * CHUNK, CHUNK), CHUNK)
-        t_high, t_low = split(col_t[slot, span, :])
-        s_high, s_low = split(col_s[slot, span, :])
+        t_high, t_low = split(col_t[:, span, :].reshape(2 * CHUNK, DT))
+        s_high, s_low = split(col_s[:, span, :].reshape(2 * CHUNK, DS))
         teacher = nt(jnp.concatenate([t_high, t_high, t_low], axis=1), row_t[xb])
         student = nt(jnp.concatenate([s_high, s_high, s_low], axis=1), row_s[xb])
-        at = pl.ds(pl.multiple_of(slot * rows + j * CHUNK, CHUNK), CHUNK)
-        t_sc[xb, at, :] = teacher
-        s_sc[xb, at, :] = student
+        for slot in range(2):
+            at = pl.ds(pl.multiple_of(slot * rows + j * CHUNK, CHUNK), CHUNK)
+            t_sc[xb, at, :] = teacher[slot * CHUNK:(slot + 1) * CHUNK]
+            s_sc[xb, at, :] = student[slot * CHUNK:(slot + 1) * CHUNK]
+        t_three = teacher.reshape(2 * CHUNK // 8, 8, rows)
+        s_three = student.reshape(2 * CHUNK // 8, 8, rows)
         t_old, s_old = acc[xb, 0], acc[xb, 3]
-        t_max = jnp.maximum(t_old, fold(teacher, jnp.max))
-        s_max = jnp.maximum(s_old, fold(student, jnp.max))
+        t_max = jnp.maximum(t_old, jnp.max(t_three, axis=0))
+        s_max = jnp.maximum(s_old, jnp.max(s_three, axis=0))
         t_scale = jnp.exp2(t_old - t_max)
         s_scale = jnp.exp2(s_old - s_max)
-        t_three = teacher.reshape(CHUNK // 8, 8, rows)
-        s_three = student.reshape(CHUNK // 8, 8, rows)
         t_exp = jnp.exp2(t_three - t_max[None])
         s_exp = jnp.exp2(s_three - s_max[None])
         acc[xb, 0] = t_max
@@ -148,50 +153,51 @@
             start = -jnp.inf if kind in (0, 3) else 0.0
             acc[xb, kind] = jnp.full((8, rows), start, jnp.float32)
 
-    def first_send():
-        for slot in range(2):
-            for way, goes in going(slot):
-                @pl.when(jnp.logical_and(goes, z == sources[slot]))
-                def _():
-                    def send(j, carry):
-                        for copy in z_copies(slot, j, way):
-                            copy.start()
-                        return carry
-                    lax.fori_loop(0, chunks, send, 0)
-
-    first_send()
     for copy in x_copies:
         copy.start()
+
+    def first_send(j, carry):
+        for slot in range(2):
+            for to in range(levels):
+                @pl.when(source_sends(slot, to))
+                def _():
+                    for copy in z_copies(slot, j, to):
+                        copy.start()
+        return carry
+
+    lax.fori_loop(0, chunks, first_send, 0)
     for load in loads:
         load.wait()
     put_rows(x, own_t[...], own_s[...])
+    half = chunks // 2
 
     def gather(j, carry):
         for slot in range(2):
             @pl.when(z != sources[slot])
             def _():
-                for copy in z_copies(slot, j, 0):
+                for copy in z_copies(slot, j, 1):
                     copy.wait_recv()
-                for way, goes in going(slot):
-                    @pl.when(goes)
+                for to in (0, last):
+                    @pl.when(forwards(slot, to))
                     def _():
-                        for copy in z_copies(slot, j, way):
+                        for copy in z_copies(slot, j, to):
                             copy.start()
-        for slot in range(2):
-            relate(x, slot, j)
+
+        relate(x, j)
+
+        @pl.when(j == half)
+        def _():
+            for copy in x_copies:
+                copy.wait_recv()
+            put_rows(1 - x, nbr_t[...], nbr_s[...])
+
+        @pl.when(j >= half)
+        def _():
+            relate(1 - x, j - half)
+            relate(1 - x, j)
         return carry
 
     lax.fori_loop(0, chunks, gather, 0)
-    for copy in x_copies:
-        copy.wait_recv()
-    put_rows(1 - x, nbr_t[...], nbr_s[...])
-
-    def second(j, carry):
-        for slot in range(2):
-            relate(1 - x, slot, j)
-        return carry
-
-    lax.fori_loop(0, chunks, second, 0)
 
     for xb in range(2):
         t_max, s_max = acc[xb, 0], acc[xb, 3]
@@ -258,9 +264,25 @@
 
     for step in range(1, levels):
         level_copy(step, z).start()
+    tiles = 2 * rows // TILE
+
+    def row_weights(xb):
+        rows_t = wide[xb, 0:1, :]
+        rows_s = wide[xb, 1:2, :]
+
+        def tile(j, carry):
+            at = pl.ds(pl.multiple_of(j * TILE, TILE), TILE)
+            w_row[xb, at, :] = jnp.exp2(s_sc[xb, at, :] - rows_s) - jnp.exp2(t_sc[xb, at, :] - rows_t)
+            return carry
+
+        lax.fori_loop(0, tiles, tile, 0)
+
+    row_weights(1 - x)
+    row_weights(x)
     for step in range(1, levels):
         level_copy(step, (z - step + levels) % levels).wait_recv()
-    columns = [level_in[source].T for source in sources]
+    for slot in range(2):
+        col_level[slot * rows:(slot + 1) * rows, :] = level_in[sources[slot]].T
 
     def part_copy(step):
         other = (place + step) % (2 * groups)
@@ -271,21 +293,20 @@
         )
 
     def gradient(xb):
-        rows_t = wide[xb, 0:1, :]
-        rows_s = wide[xb, 1:2, :]
-        for slot in range(2):
-            for j in range(chunks):
-                at = slice(slot * rows + j * CHUNK, slot * rows + (j + 1) * CHUNK)
-                col = columns[slot][j * CHUNK:(j + 1) * CHUNK]
-                teacher = t_sc[xb, at, :]
-                student = s_sc[xb, at, :]
-                weight = (
-                    jnp.exp2(student - rows_s) + jnp.exp2(student - col[:, 1:2])
-                    - jnp.exp2(teacher - rows_t) - jnp.exp2(teacher - col[:, 0:1])
-                )
-                high_part, low_part = split(weight)
-                w_high[at, :] = high_part
-                w_low[at, :] = low_part
+        def tile(j, carry):
+            at = pl.ds(pl.multiple_of(j * TILE, TILE), TILE)
+            col = col_level[at, :]
+            weight = (
+                w_row[xb, at, :]
+                + jnp.exp2(s_sc[xb, at, :] - col[:, 1:2])
+                - jnp.exp2(t_sc[xb, at, :] - col[:, 0:1])
+            )
+            high_part, low_part = split(weight)
+            w_high[at, :] = high_part
+            w_low[at, :] = low_part
+            return carry
+
+        lax.fori_loop(0, tiles, tile, 0)
         first = nn(q_tr[...], w_high[...])
         part[xb] = first[:DS] + first[DS:] + nn(q_tr[0:DS, :], w_low[...])
 
@@ -333,15 +354,21 @@
     )
     for copy in x_copies:
         copy.wait_send()
-    for slot in range(2):
-        for way, goes in going(slot):
-            @pl.when(goes)
-            def _():
-                def done(j, carry):
-                    for copy in z_copies(slot, j, way):
+
+    def sent(j, carry):
+        for slot in range(2):
+            for to in range(levels):
+                goes = source_sends(slot, to)
+                if to in (0, last):
+                    goes = jnp.logical_or(goes, forwards(slot, to))
+
+                @pl.when(goes)
+                def _():
+                    for copy in z_copies(slot, j, to):
                         copy.wait_send()
-                    return carry
-                lax.fori_loop(0, chunks, done, 0)
+        return carry
+
+    lax.fori_loop(0, chunks, sent, 0)
     for step in range(1, 2 * groups):
         stat_copy(step).wait_send()
         part_copy(step).wait_send()
@@ -389,6 +416,8 @@
                 pltpu.VMEM((2 * groups, 2, 8, rows), f32),
                 pltpu.VMEM((levels, 8, rows), f32),
                 pltpu.VMEM((2, 2, rows), f32),
+                pltpu.VMEM((2 * rows, 8), f32),
+                pltpu.VMEM((2, 2 * rows, rows), f32),
                 pltpu.VMEM((2 * DS, 2 * rows), bf16),
                 pltpu.VMEM((2 * rows, rows), bf16),
                 pltpu.VMEM((2 * rows, rows), bf16),
@@ -399,7 +428,7 @@
                 dma((2, 2)),
                 dma((2,)),
                 dma((2,)),
-                dma((2, 2, chunks, 2)),
+                dma((levels, 2, chunks, 2)),
                 dma((2, chunks, 2)),
                 dma((2 * groups,)),
                 dma((2 * groups,)),
@@ -411,7 +440,7 @@
                 dma((2,)),
             ],
             compiler_params=pltpu.CompilerParams(
-                collective_id=0, has_side_effects=True, vmem_limit_bytes=48 * 1024 * 1024
+                collective_id=0, has_side_effects=True, vmem_limit_bytes=60 * 1024 * 1024
             ),
         )(teacher_q, student_q)
         return grad, loss.reshape(())

time: 87 us -> 52.6 us (0.60)
  Pallas kernels: 81.5 us -> 47.7 us
  local copies, waits for them, and re-layouts: 2.87 us -> 1.77 us
    pallas_call x1, Pallas kernels: 81.5 us -> 47.7 us  [shards(): pl.pallas_call(functools.partial(kernel, groups, levels, rows, batches),...]
    unnamed x5 -> x1, local copies, waits for them, and re-layouts: 2.87 us -> 1.77 us
where the time goes in v2:
time: 52.6 us; the launch traced here: 51.8 us
  Pallas kernels  47.7 us (91%)
  between operations  2.39 us (5%)
  local copies, waits for them, and re-layouts  1.77 us (3%)
    pallas_call x1, Pallas kernels, shards(): pl.pallas_call(functools.partial(kernel, groups, levels, rows, batches),...  47.7 us
    unnamed x1, local copies, waits for them, and re-layouts  1.77 us

profile of v2, /device:TPU:0, one launch (start us, length us, event | category | flops | bytes accessed | tf_op | source)
XLA Modules:
  0.0 51.8 jit_solution(1919007419984588354)
XLA Ops:
  0.6 47.7 %shard_map.41 = (f32[2,384,128]{2,1,0:T(8,128)}, f32[1,1]{1,0:T(1,128)}) custom-call(f32[2,384,256]{2,1,0:T(8,128)} %t_hbm.1, f32[2,384,128]{2,1,0:T(8,128)} %s_hbm.1), custom_call_target="tpu_custom_call" | custom-call | tf_op jit(solution)/shard_map/pallas_call | solution.py:393
  48.3 1.8 %copy.6 = f32[2,384,128]{2,1,0:T(8,128)} copy(f32[2,384,128]{2,1,0:T(8,128)} %get-tuple-element.8) | data formatting | bytes 786432

commit v3 on v2

--- a/solution.py
+++ b/solution.py
@@ -11,7 +11,8 @@
 HEADS = 1
 DT = 256
 DS = 128
-CHUNK = 96
+CHUNK = 64
+LANES = 128
 TILE = 64
 MESH = pl.DeviceIdType.MESH
 LOG2E = 1.4426950408889634
@@ -38,10 +39,11 @@
     groups, levels, rows, batches,
     t_hbm, s_hbm, out_ref, loss_ref,
     own_t, own_s, nbr_t, nbr_s, col_t, col_s, row_t, row_s, t_sc, s_sc, acc,
-    stat_in, level_in, wide, col_level, w_row, q_tr, w_high, w_low, part, part_in, total_in,
+    stat_in, stat_col, div_in, wide, col_level, w_row, q_tr, w_high, w_low,
+    part, x_in, x_sum, y_in, total_in,
     load_sem, slot_sem, x_send, x_recv, z_send, z_recv,
-    stat_send, stat_recv, level_send, level_recv, part_send, part_recv,
-    out_send, out_recv,
+    stat_send, stat_recv, col_send, col_recv, div_send, div_recv,
+    px_send, px_recv, py_send, py_recv, out_send, out_recv, total_send, total_recv,
 ):
     chunks = rows // CHUNK
     pb = lax.axis_index("pb")
@@ -62,10 +64,19 @@
         other = (place + step) % (2 * groups)
         planes.append(((other % groups) * batches + seq, z * 2 + other // groups))
     line = [(pb, ((z + step) % levels) * 2 + x) for step in range(1, levels)]
-    everyone = planes + line + [(mate, ka)]
     barrier = pltpu.get_barrier_semaphore()
-    for device in everyone:
+    count = 2 * groups * levels
+    index = place * levels + z
+
+    def greet(step, carry):
+        other = (index + step) % count
+        spot, level = other // levels, other % levels
+        device = ((spot % groups) * batches + seq, level * 2 + spot // groups)
         pl.semaphore_signal(barrier, inc=1, device_id=device, device_id_type=MESH)
+        return carry
+
+    lax.fori_loop(1, count, greet, 0)
+    pl.semaphore_signal(barrier, inc=1, device_id=(mate, ka), device_id_type=MESH)
 
     loads = [
         pltpu.make_async_copy(t_hbm.at[seq], own_t, load_sem.at[0]),
@@ -78,7 +89,7 @@
             pltpu.make_async_copy(s_hbm.at[seq], col_s.at[slot], slot_sem.at[slot, 1]).start()
     for load in loads:
         load.start()
-    pl.semaphore_wait(barrier, len(everyone))
+    pl.semaphore_wait(barrier, count)
 
     x_copies = [
         pltpu.make_async_remote_copy(
@@ -172,6 +183,16 @@
     half = chunks // 2
 
     def gather(j, carry):
+        @pl.when(j == half)
+        def _():
+            for copy in x_copies:
+                copy.wait_recv()
+            put_rows(1 - x, nbr_t[...], nbr_s[...])
+
+        @pl.when(j >= half)
+        def _():
+            relate(1 - x, j - half)
+
         for slot in range(2):
             @pl.when(z != sources[slot])
             def _():
@@ -185,15 +206,8 @@
 
         relate(x, j)
 
-        @pl.when(j == half)
-        def _():
-            for copy in x_copies:
-                copy.wait_recv()
-            put_rows(1 - x, nbr_t[...], nbr_s[...])
-
         @pl.when(j >= half)
         def _():
-            relate(1 - x, j - half)
             relate(1 - x, j)
         return carry
 
@@ -227,6 +241,20 @@
             device_id=planes[step - 1], device_id_type=MESH,
         )
 
+    near = jnp.minimum(z, levels - 1 - z)
+    user = jnp.where(seq == 0, near, groups - 1 - near)
+    my_slot = jnp.where(z == near, 0, 1)
+
+    def col_copy(xb, step):
+        return pltpu.make_async_remote_copy(
+            src_ref=stat_in.at[place, xb], dst_ref=stat_col.at[my_slot, place],
+            send_sem=col_send.at[xb, step], recv_sem=col_recv.at[my_slot, place],
+            device_id=(user * batches + seq, ((z + step) % levels) * 2 + xb), device_id_type=MESH,
+        )
+
+    for step in range(1, levels):
+        for xb in range(2):
+            col_copy(xb, step).start()
     for step in range(1, 2 * groups):
         stat_copy(step).start()
     for slot in range(2):
@@ -236,34 +264,36 @@
     for step in range(1, 2 * groups):
         stat_wait(step).wait_recv()
 
-    t_max = stat_in[0, :, 0:1, :]
-    s_max = stat_in[0, :, 3:4, :]
-    for other in range(1, 2 * groups):
-        t_max = jnp.maximum(t_max, stat_in[other, :, 0:1, :])
-        s_max = jnp.maximum(s_max, stat_in[other, :, 3:4, :])
-    t_sum = cross = s_sum = jnp.zeros((2, 1, rows), jnp.float32)
-    for other in range(2 * groups):
-        t_scale = jnp.exp2(stat_in[other, :, 0:1, :] - t_max)
-        s_scale = jnp.exp2(stat_in[other, :, 3:4, :] - s_max)
-        t_sum = t_sum + stat_in[other, :, 1:2, :] * t_scale
-        cross = cross + stat_in[other, :, 2:3, :] * t_scale
-        s_sum = s_sum + stat_in[other, :, 4:5, :] * s_scale
-    t_level = t_max + jnp.log2(t_sum)
-    s_level = s_max + jnp.log2(s_sum)
-    divergence = LN2 * (cross / t_sum - t_level + s_level)
-    both = jnp.broadcast_to(jnp.sum(divergence, axis=0), (6, rows))
-    wide[...] = jnp.concatenate([t_level, s_level], axis=1)
-    level_in[z] = jnp.concatenate([wide[x], both], axis=0)
-
-    def level_copy(step, slot):
-        return pltpu.make_async_remote_copy(
-            src_ref=level_in.at[slot], dst_ref=level_in.at[slot],
-            send_sem=level_send.at[step], recv_sem=level_recv.at[step],
+    def combine(stats):
+        t_max = functools.reduce(jnp.maximum, [stat[0:1] for stat in stats])
+        s_max = functools.reduce(jnp.maximum, [stat[3:4] for stat in stats])
+        t_sum = cross = s_sum = jnp.zeros((1, rows), jnp.float32)
+        for stat in stats:
+            t_scale = jnp.exp2(stat[0:1] - t_max)
+            t_sum = t_sum + stat[1:2] * t_scale
+            cross = cross + stat[2:3] * t_scale
+            s_sum = s_sum + stat[4:5] * jnp.exp2(stat[3:4] - s_max)
+        t_level = t_max + jnp.log2(t_sum)
+        s_level = s_max + jnp.log2(s_sum)
+        return t_level, s_level, LN2 * (cross / t_sum - t_level + s_level)
+
+    divergence = jnp.zeros((1, rows), jnp.float32)
+    for xb in range(2):
+        t_level, s_level, share = combine([stat_in[other, xb] for other in range(2 * groups)])
+        wide[xb] = jnp.concatenate([t_level, s_level], axis=0)
+        divergence = divergence + share
+    div_in[z] = jnp.broadcast_to(divergence, (8, rows))
+
+    def div_copy(step, slot):
+        return pltpu.make_async_remote_copy(
+            src_ref=div_in.at[slot], dst_ref=div_in.at[slot],
+            send_sem=div_send.at[step], recv_sem=div_recv.at[step],
             device_id=line[step - 1], device_id_type=MESH,
         )
 
     for step in range(1, levels):
-        level_copy(step, z).start()
+        div_copy(step, z).start()
+
     tiles = 2 * rows // TILE
 
     def row_weights(xb):
@@ -279,17 +309,54 @@
 
     row_weights(1 - x)
     row_weights(x)
-    for step in range(1, levels):
-        level_copy(step, (z - step + levels) % levels).wait_recv()
     for slot in range(2):
-        col_level[slot * rows:(slot + 1) * rows, :] = level_in[sources[slot]].T
-
-    def part_copy(step):
-        other = (place + step) % (2 * groups)
-        return pltpu.make_async_remote_copy(
-            src_ref=part.at[other // groups], dst_ref=part_in.at[step],
-            send_sem=part_send.at[step], recv_sem=part_recv.at[step],
-            device_id=planes[step - 1], device_id_type=MESH,
+        @pl.when(z == sources[slot])
+        def _():
+            for other in range(2 * groups):
+                stat_col[slot, other] = stat_in[other, x]
+
+        @pl.when(z != sources[slot])
+        def _():
+            for other in range(2 * groups):
+                pltpu.make_async_remote_copy(
+                    src_ref=stat_col.at[slot, other], dst_ref=stat_col.at[slot, other],
+                    send_sem=col_send.at[0, 0], recv_sem=col_recv.at[slot, other],
+                    device_id=x_device, device_id_type=MESH,
+                ).wait_recv()
+
+        t_level, s_level, _ = combine([stat_col[slot, other] for other in range(2 * groups)])
+        both = jnp.concatenate([t_level, s_level, jnp.zeros((6, rows), jnp.float32)], axis=0)
+        col_level[slot * rows:(slot + 1) * rows, :] = both.T
+
+    blocks = rows // LANES
+
+    def px_copy(b):
+        return pltpu.make_async_remote_copy(
+            src_ref=part.at[1 - x, b], dst_ref=x_in.at[b],
+            send_sem=px_send.at[b], recv_sem=px_recv.at[b],
+            device_id=x_device, device_id_type=MESH,
+        )
+
+    def py_copy(step, b):
+        return pltpu.make_async_remote_copy(
+            src_ref=x_sum.at[b], dst_ref=y_in.at[step, b],
+            send_sem=py_send.at[step, b], recv_sem=py_recv.at[step, b],
+            device_id=(((y + step) % groups) * batches + seq, ka), device_id_type=MESH,
+        )
+
+    def out_copy(which, b):
+        span = pl.ds(b * LANES, LANES)
+        return pltpu.make_async_remote_copy(
+            src_ref=out_ref.at[which, span, :], dst_ref=out_ref.at[which, span, :],
+            send_sem=out_send.at[b], recv_sem=out_recv.at[b],
+            device_id=(mate, ka), device_id_type=MESH,
+        )
+
+    def total_copy(which):
+        return pltpu.make_async_remote_copy(
+            src_ref=total_in.at[which], dst_ref=total_in.at[which],
+            send_sem=total_send, recv_sem=total_recv,
+            device_id=(mate, ka), device_id_type=MESH,
         )
 
     def gradient(xb):
@@ -308,50 +375,38 @@
 
         lax.fori_loop(0, tiles, tile, 0)
         first = nn(q_tr[...], w_high[...])
-        part[xb] = first[:DS] + first[DS:] + nn(q_tr[0:DS, :], w_low[...])
+        product = first[:DS] + first[DS:] + nn(q_tr[0:DS, :], w_low[...])
+        for b in range(blocks):
+            part[xb, b] = product[:, b * LANES:(b + 1) * LANES]
 
     gradient(1 - x)
-    for step in range(1, 2 * groups):
-        other = (place + step) % (2 * groups)
-        @pl.when(other // groups != x)
-        def _():
-            part_copy(step).start()
+    for b in range(blocks):
+        px_copy(b).start()
     gradient(x)
-    for step in range(1, 2 * groups):
-        other = (place + step) % (2 * groups)
-        @pl.when(other // groups == x)
-        def _():
-            part_copy(step).start()
-    total = level_in[0, 2:3, :]
+    for b in range(blocks):
+        px_copy(b).wait_recv()
+        x_sum[b] = part[x, b] + x_in[b]
+        for step in range(1, groups):
+            py_copy(step, b).start()
+    for step in range(1, levels):
+        div_copy(step, (z - step + levels) % levels).wait_recv()
+    total = div_in[0, 0:1, :]
     for level in range(1, levels):
-        total = total + level_in[level, 2:3, :]
+        total = total + div_in[level, 0:1, :]
     total_in[seq] = jnp.broadcast_to(total, (8, rows))
-    total_copy = pltpu.make_async_remote_copy(
-        src_ref=total_in.at[seq], dst_ref=total_in.at[seq],
-        send_sem=out_send.at[1], recv_sem=out_recv.at[1],
-        device_id=(mate, ka), device_id_type=MESH,
-    )
-    total_copy.start()
-    result = part[x]
-    for step in range(1, 2 * groups):
-        part_copy(step).wait_recv()
-        result = result + part_in[step]
-    out_ref[seq] = result.T
-    out_copy = pltpu.make_async_remote_copy(
-        src_ref=out_ref.at[seq], dst_ref=out_ref.at[seq],
-        send_sem=out_send.at[0], recv_sem=out_recv.at[0],
-        device_id=(mate, ka), device_id_type=MESH,
-    )
-    out_copy.start()
-    total_copy.wait_send()
-    pltpu.make_async_remote_copy(
-        src_ref=total_in.at[1 - seq], dst_ref=total_in.at[1 - seq],
-        send_sem=out_send.at[1], recv_sem=out_recv.at[1],
-        device_id=(mate, ka), device_id_type=MESH,
-    ).wait_recv()
+    total_copy(seq).start()
+    for b in range(blocks):
+        result = x_sum[b]
+        for step in range(1, groups):
+            py_copy(step, b).wait_recv()
+            result = result + y_in[step, b]
+        out_ref[seq, b * LANES:(b + 1) * LANES, :] = result.T
+        out_copy(seq, b).start()
+    total_copy(1 - seq).wait_recv()
     loss_ref[0, 0] = jnp.sum(total_in[0, 0:1, :] + total_in[1, 0:1, :]) / (
         batches * HEADS * rows * 2 * levels
     )
+    total_copy(seq).wait_send()
     for copy in x_copies:
         copy.wait_send()
 
@@ -371,15 +426,16 @@
     lax.fori_loop(0, chunks, sent, 0)
     for step in range(1, 2 * groups):
         stat_copy(step).wait_send()
-        part_copy(step).wait_send()
     for step in range(1, levels):
-        level_copy(step, z).wait_send()
-    out_copy.wait_send()
-    pltpu.make_async_remote_copy(
-        src_ref=out_ref.at[1 - seq], dst_ref=out_ref.at[1 - seq],
-        send_sem=out_send.at[0], recv_sem=out_recv.at[0],
-        device_id=(mate, ka), device_id_type=MESH,
-    ).wait_recv()
+        div_copy(step, z).wait_send()
+        for xb in range(2):
+            col_copy(xb, step).wait_send()
+    for b in range(blocks):
+        px_copy(b).wait_send()
+        for step in range(1, groups):
+            py_copy(step, b).wait_send()
+        out_copy(seq, b).wait_send()
+        out_copy(1 - seq, b).wait_recv()
 
 
 def solution(mesh):
@@ -388,6 +444,7 @@
         groups = mesh.shape["pb"] // batches
         levels = mesh.shape["ka"] // 2
         chunks = rows // CHUNK
+        blocks = rows // LANES
         f32, bf16 = jnp.float32, jnp.bfloat16
         dma = pltpu.SemaphoreType.DMA
         grad, loss = pl.pallas_call(
@@ -414,6 +471,7 @@
                 pltpu.VMEM((2, 2 * rows, rows), f32),
                 pltpu.VMEM((2, 5, 8, rows), f32),
                 pltpu.VMEM((2 * groups, 2, 8, rows), f32),
+                pltpu.VMEM((2, 2 * groups, 8, rows), f32),
                 pltpu.VMEM((levels, 8, rows), f32),
                 pltpu.VMEM((2, 2, rows), f32),
                 pltpu.VMEM((2 * rows, 8), f32),
@@ -421,8 +479,10 @@
                 pltpu.VMEM((2 * DS, 2 * rows), bf16),
                 pltpu.VMEM((2 * rows, rows), bf16),
                 pltpu.VMEM((2 * rows, rows), bf16),
-                pltpu.VMEM((2, DS, rows), f32),
-                pltpu.VMEM((2 * groups, DS, rows), f32),
+                pltpu.VMEM((2, blocks, DS, LANES), f32),
+                pltpu.VMEM((blocks, DS, LANES), f32),
+                pltpu.VMEM((blocks, DS, LANES), f32),
+                pltpu.VMEM((groups, blocks, DS, LANES), f32),
                 pltpu.VMEM((batches, 8, rows), f32),
                 dma((2,)),
                 dma((2, 2)),
@@ -432,12 +492,18 @@
                 dma((2, chunks, 2)),
                 dma((2 * groups,)),
                 dma((2 * groups,)),
+                dma((2, levels)),
+                dma((2, 2 * groups)),
                 dma((levels,)),
                 dma((levels,)),
-                dma((2 * groups,)),
-                dma((2 * groups,)),
-                dma((2,)),
-                dma((2,)),
+                dma((blocks,)),
+                dma((blocks,)),
+                dma((groups, blocks)),
+                dma((groups, blocks)),
+                dma((blocks,)),
+                dma((blocks,)),
+                dma,
+                dma,
             ],
             compiler_params=pltpu.CompilerParams(
                 collective_id=0, has_side_effects=True, vmem_limit_bytes=60 * 1024 * 1024

time: 52.6 us -> 53.5 us (1.017); the launches traced: 51.8 us -> 53.3 us
  Pallas kernels: 47.7 us -> 49.2 us
    pallas_call x1, Pallas kernels: 47.7 us -> 49.2 us  [shards(): pl.pallas_call(functools.partial(kernel, groups, levels, rows, batches),...]
where the time goes in v3:
time: 53.5 us; the launch traced here: 53.3 us
  Pallas kernels  49.2 us (92%)
  between operations  2.39 us (4%)
  local copies, waits for them, and re-layouts  1.77 us (3%)
    pallas_call x1, Pallas kernels, shards(): pl.pallas_call(functools.partial(kernel, groups, levels, rows, batches),...  49.2 us
    unnamed x1, local copies, waits for them, and re-layouts  1.77 us

profile of v3, /device:TPU:0, one launch (start us, length us, event | category | flops | bytes accessed | tf_op | source)
XLA Modules:
  0.0 53.3 jit_solution(16981151070338886773)
XLA Ops:
  0.6 49.2 %shard_map.41 = (f32[2,384,128]{2,1,0:T(8,128)}, f32[1,1]{1,0:T(1,128)}) custom-call(f32[2,384,256]{2,1,0:T(8,128)} %t_hbm.1, f32[2,384,128]{2,1,0:T(8,128)} %s_hbm.1), custom_call_target="tpu_custom_call" | custom-call | tf_op jit(solution)/shard_map/pallas_call | solution.py:450
  49.8 1.8 %copy.6 = f32[2,384,128]{2,1,0:T(8,128)} copy(f32[2,384,128]{2,1,0:T(8,128)} %get-tuple-element.8) | data formatting | bytes 786432

commit v4 on v3

--- a/solution.py
+++ b/solution.py
@@ -11,9 +11,10 @@
 HEADS = 1
 DT = 256
 DS = 128
-CHUNK = 64
+CHUNK = 96
 LANES = 128
 TILE = 64
+PART = 32
 MESH = pl.DeviceIdType.MESH
 LOG2E = 1.4426950408889634
 LN2 = 0.6931471805599453
@@ -23,12 +24,6 @@
     high = values.astype(jnp.bfloat16)
     low = (values - high.astype(jnp.float32)).astype(jnp.bfloat16)
     return high, low
-
-
-def nt(left, right):
-    return lax.dot_general(
-        left, right, (((1,), (1,)), ((), ())), preferred_element_type=jnp.float32
-    )
 
 
 def nn(left, right):
@@ -129,35 +124,50 @@
         return jnp.logical_and(z == beside, waits)
 
     def put_rows(xb, teacher, student):
-        t_high, t_low = split(teacher * (LOG2E / math.sqrt(DT)))
-        s_high, s_low = split(student * (LOG2E / math.sqrt(DS)))
-        row_t[xb] = jnp.concatenate([t_high, t_low, t_high], axis=1)
-        row_s[xb] = jnp.concatenate([s_high, s_low, s_high], axis=1)
+        t_high, t_low = split((teacher * (LOG2E / math.sqrt(DT))).T)
+        s_high, s_low = split((student * (LOG2E / math.sqrt(DS))).T)
+        for part_index, (t_part, s_part) in enumerate(
+            ((t_high, s_high), (t_low, s_low), (t_high, s_high))
+        ):
+            row_t[xb, part_index * DT:(part_index + 1) * DT, :] = t_part
+            row_s[xb, part_index * DS:(part_index + 1) * DS, :] = s_part
 
     def relate(xb, j):
         span = pl.ds(pl.multiple_of(j * CHUNK, CHUNK), CHUNK)
         t_high, t_low = split(col_t[:, span, :].reshape(2 * CHUNK, DT))
         s_high, s_low = split(col_s[:, span, :].reshape(2 * CHUNK, DS))
-        teacher = nt(jnp.concatenate([t_high, t_high, t_low], axis=1), row_t[xb])
-        student = nt(jnp.concatenate([s_high, s_high, s_low], axis=1), row_s[xb])
+        teacher = nn(jnp.concatenate([t_high, t_high, t_low], axis=1), row_t[xb])
+        student = nn(jnp.concatenate([s_high, s_high, s_low], axis=1), row_s[xb])
+        tiles = []
         for slot in range(2):
-            at = pl.ds(pl.multiple_of(slot * rows + j * CHUNK, CHUNK), CHUNK)
+            base = slot * rows + j * CHUNK
+            at = pl.ds(pl.multiple_of(base, CHUNK), CHUNK)
             t_sc[xb, at, :] = teacher[slot * CHUNK:(slot + 1) * CHUNK]
             s_sc[xb, at, :] = student[slot * CHUNK:(slot + 1) * CHUNK]
-        t_three = teacher.reshape(2 * CHUNK // 8, 8, rows)
-        s_three = student.reshape(2 * CHUNK // 8, 8, rows)
+            tiles += [pl.ds(pl.multiple_of(base + i * PART, PART), PART) for i in range(CHUNK // PART)]
+
+        def read(ref, at):
+            return ref[xb, at, :].reshape(PART // 8, 8, rows)
+
         t_old, s_old = acc[xb, 0], acc[xb, 3]
-        t_max = jnp.maximum(t_old, jnp.max(t_three, axis=0))
-        s_max = jnp.maximum(s_old, jnp.max(s_three, axis=0))
+        t_max, s_max = t_old, s_old
+        for at in tiles:
+            t_max = jnp.maximum(t_max, jnp.max(read(t_sc, at), axis=0))
+            s_max = jnp.maximum(s_max, jnp.max(read(s_sc, at), axis=0))
         t_scale = jnp.exp2(t_old - t_max)
         s_scale = jnp.exp2(s_old - s_max)
-        t_exp = jnp.exp2(t_three - t_max[None])
-        s_exp = jnp.exp2(s_three - s_max[None])
+        t_sum, cross, s_sum = acc[xb, 1] * t_scale, acc[xb, 2] * t_scale, acc[xb, 4] * s_scale
+        for at in tiles:
+            t_tile, s_tile = read(t_sc, at), read(s_sc, at)
+            t_exp = jnp.exp2(t_tile - t_max[None])
+            t_sum = t_sum + jnp.sum(t_exp, axis=0)
+            cross = cross + jnp.sum(t_exp * (t_tile - s_tile), axis=0)
+            s_sum = s_sum + jnp.sum(jnp.exp2(s_tile - s_max[None]), axis=0)
         acc[xb, 0] = t_max
-        acc[xb, 1] = acc[xb, 1] * t_scale + jnp.sum(t_exp, axis=0)
-        acc[xb, 2] = acc[xb, 2] * t_scale + jnp.sum(t_exp * (t_three - s_three), axis=0)
+        acc[xb, 1] = t_sum
+        acc[xb, 2] = cross
         acc[xb, 3] = s_max
-        acc[xb, 4] = acc[xb, 4] * s_scale + jnp.sum(s_exp, axis=0)
+        acc[xb, 4] = s_sum
 
     for xb in range(2):
         for kind in range(5):
@@ -465,8 +475,8 @@
                 pltpu.VMEM((rows, DS), f32),
                 pltpu.VMEM((2, rows, DT), f32),
                 pltpu.VMEM((2, rows, DS), f32),
-                pltpu.VMEM((2, rows, 3 * DT), bf16),
-                pltpu.VMEM((2, rows, 3 * DS), bf16),
+                pltpu.VMEM((2, 3 * DT, rows), bf16),
+                pltpu.VMEM((2, 3 * DS, rows), bf16),
                 pltpu.VMEM((2, 2 * rows, rows), f32),
                 pltpu.VMEM((2, 2 * rows, rows), f32),
                 pltpu.VMEM((2, 5, 8, rows), f32),

time: 53.5 us -> 52.8 us (0.987)
  Pallas kernels: 49.2 us -> 48.4 us
    pallas_call x1, Pallas kernels: 49.2 us -> 48.4 us  [shards(): pl.pallas_call(functools.partial(kernel, groups, levels, rows, batches),...]
where the time goes in v4:
time: 52.8 us; the launch traced here: 52.6 us
  Pallas kernels  48.4 us (92%)
  between operations  2.39 us (5%)
  local copies, waits for them, and re-layouts  1.77 us (3%)
    pallas_call x1, Pallas kernels, shards(): pl.pallas_call(functools.partial(kernel, groups, levels, rows, batches),...  48.4 us
    unnamed x1, local copies, waits for them, and re-layouts  1.77 us

profile of v4, /device:TPU:0, one launch (start us, length us, event | category | flops | bytes accessed | tf_op | source)
XLA Modules:
  0.0 52.6 jit_solution(7666682469415466834)
XLA Ops:
  0.6 48.4 %shard_map.41 = (f32[2,384,128]{2,1,0:T(8,128)}, f32[1,1]{1,0:T(1,128)}) custom-call(f32[2,384,256]{2,1,0:T(8,128)} %t_hbm.1, f32[2,384,128]{2,1,0:T(8,128)} %s_hbm.1), custom_call_target="tpu_custom_call" | custom-call | tf_op jit(solution)/shard_map/pallas_call | solution.py:460
  49.1 1.8 %copy.6 = f32[2,384,128]{2,1,0:T(8,128)} copy(f32[2,384,128]{2,1,0:T(8,128)} %get-tuple-element.8) | data formatting | bytes 786432

commit v5 on v4

--- a/solution.py
+++ b/solution.py
@@ -33,7 +33,7 @@
 def kernel(
     groups, levels, rows, batches,
     t_hbm, s_hbm, out_ref, loss_ref,
-    own_t, own_s, nbr_t, nbr_s, col_t, col_s, row_t, row_s, t_sc, s_sc, acc,
+    in_t, in_s, col_t, col_s, row_t, row_s, t_sc, s_sc, acc,
     stat_in, stat_col, div_in, wide, col_level, w_row, q_tr, w_high, w_low,
     part, x_in, x_sum, y_in, total_in,
     load_sem, slot_sem, x_send, x_recv, z_send, z_recv,
@@ -74,8 +74,8 @@
     pl.semaphore_signal(barrier, inc=1, device_id=(mate, ka), device_id_type=MESH)
 
     loads = [
-        pltpu.make_async_copy(t_hbm.at[seq], own_t, load_sem.at[0]),
-        pltpu.make_async_copy(s_hbm.at[seq], own_s, load_sem.at[1]),
+        pltpu.make_async_copy(t_hbm.at[seq], in_t.at[0], load_sem.at[0]),
+        pltpu.make_async_copy(s_hbm.at[seq], in_s.at[0], load_sem.at[1]),
     ]
     for slot in range(2):
         @pl.when(z == sources[slot])
@@ -91,7 +91,7 @@
             src_ref=src.at[seq], dst_ref=dst, send_sem=x_send.at[i], recv_sem=x_recv.at[i],
             device_id=x_device, device_id_type=MESH,
         )
-        for i, (src, dst) in enumerate(((t_hbm, nbr_t), (s_hbm, nbr_s)))
+        for i, (src, dst) in enumerate(((t_hbm, in_t.at[1]), (s_hbm, in_s.at[1])))
     ]
 
     def z_copies(slot, j, to):
@@ -187,22 +187,9 @@
         return carry
 
     lax.fori_loop(0, chunks, first_send, 0)
-    for load in loads:
-        load.wait()
-    put_rows(x, own_t[...], own_s[...])
     half = chunks // 2
 
-    def gather(j, carry):
-        @pl.when(j == half)
-        def _():
-            for copy in x_copies:
-                copy.wait_recv()
-            put_rows(1 - x, nbr_t[...], nbr_s[...])
-
-        @pl.when(j >= half)
-        def _():
-            relate(1 - x, j - half)
-
+    def arrive(j):
         for slot in range(2):
             @pl.when(z != sources[slot])
             def _():
@@ -214,14 +201,35 @@
                         for copy in z_copies(slot, j, to):
                             copy.start()
 
-        relate(x, j)
-
-        @pl.when(j >= half)
-        def _():
-            relate(1 - x, j)
+    def gather(k, carry):
+        late = k - half
+        phase = jnp.where(k < half, 1, late % 3)
+        j = jnp.where(k < half, k, late // 3 + jnp.where(phase == 0, 0, half))
+        own = phase == 1
+
+        @pl.when(k == 0)
+        def _():
+            for load in loads:
+                load.wait()
+
+        @pl.when(k == half)
+        def _():
+            for copy in x_copies:
+                copy.wait_recv()
+
+        @pl.when(jnp.logical_or(k == 0, k == half))
+        def _():
+            which = jnp.where(k == 0, 0, 1)
+            put_rows(jnp.where(k == 0, x, 1 - x), in_t[which], in_s[which])
+
+        @pl.when(own)
+        def _():
+            arrive(j)
+
+        relate(jnp.where(own, x, 1 - x), j)
         return carry
 
-    lax.fori_loop(0, chunks, gather, 0)
+    lax.fori_loop(0, 2 * chunks, gather, 0)
 
     for xb in range(2):
         t_max, s_max = acc[xb, 0], acc[xb, 3]
@@ -317,8 +325,11 @@
 
         lax.fori_loop(0, tiles, tile, 0)
 
-    row_weights(1 - x)
-    row_weights(x)
+    def both_weights(xb, carry):
+        row_weights(xb)
+        return carry
+
+    lax.fori_loop(0, 2, both_weights, 0)
     for slot in range(2):
         @pl.when(z == sources[slot])
         def _():
@@ -389,10 +400,16 @@
         for b in range(blocks):
             part[xb, b] = product[:, b * LANES:(b + 1) * LANES]
 
-    gradient(1 - x)
-    for b in range(blocks):
-        px_copy(b).start()
-    gradient(x)
+    def both_gradients(step, carry):
+        gradient(jnp.where(step == 0, 1 - x, x))
+
+        @pl.when(step == 0)
+        def _():
+            for b in range(blocks):
+                px_copy(b).start()
+        return carry
+
+    lax.fori_loop(0, 2, both_gradients, 0)
     for b in range(blocks):
         px_copy(b).wait_recv()
         x_sum[b] = part[x, b] + x_in[b]
@@ -469,10 +486,8 @@
                 pl.BlockSpec(memory_space=pltpu.SMEM),
             ),
             scratch_shapes=[
-                pltpu.VMEM((rows, DT), f32),
-                pltpu.VMEM((rows, DS), f32),
-                pltpu.VMEM((rows, DT), f32),
-                pltpu.VMEM((rows, DS), f32),
+                pltpu.VMEM((2, rows, DT), f32),
+                pltpu.VMEM((2, rows, DS), f32),
                 pltpu.VMEM((2, rows, DT), f32),
                 pltpu.VMEM((2, rows, DS), f32),
                 pltpu.VMEM((2, 3 * DT, rows), bf16),

time: 52.8 us -> 52.8 us (level)
  no operation moved by 1% of the time
where the time goes in v5:
time: 52.8 us; the launch traced here: 52.6 us
  Pallas kernels  48.5 us (92%)
  between operations  2.39 us (5%)
  local copies, waits for them, and re-layouts  1.77 us (3%)
    pallas_call x1, Pallas kernels, shards(): pl.pallas_call(functools.partial(kernel, groups, levels, rows, batches),...  48.5 us
    unnamed x1, local copies, waits for them, and re-layouts  1.77 us

profile of v5, /device:TPU:0, one launch (start us, length us, event | category | flops | bytes accessed | tf_op | source)
XLA Modules:
  0.0 52.6 jit_solution(5485436002060820860)
XLA Ops:
  0.6 48.5 %shard_map.41 = (f32[2,384,128]{2,1,0:T(8,128)}, f32[1,1]{1,0:T(1,128)}) custom-call(f32[2,384,256]{2,1,0:T(8,128)} %t_hbm.1, f32[2,384,128]{2,1,0:T(8,128)} %s_hbm.1), custom_call_target="tpu_custom_call" | custom-call | tf_op jit(solution)/shard_map/pallas_call | solution.py:477
  49.1 1.8 %copy.6 = f32[2,384,128]{2,1,0:T(8,128)} copy(f32[2,384,128]{2,1,0:T(8,128)} %get-tuple-element.8) | data formatting | bytes 786432

commit v6 on v5

--- a/solution.py
+++ b/solution.py
@@ -24,6 +24,12 @@
     high = values.astype(jnp.bfloat16)
     low = (values - high.astype(jnp.float32)).astype(jnp.bfloat16)
     return high, low
+
+
+def nt(left, right):
+    return lax.dot_general(
+        left, right, (((1,), (1,)), ((), ())), preferred_element_type=jnp.float32
+    )
 
 
 def nn(left, right):
@@ -465,6 +471,602 @@
         out_copy(1 - seq, b).wait_recv()
 
 
+def folded_kernel(
+    groups, levels, rows, batches,
+    t_hbm, s_hbm, out_ref, loss_ref,
+    in_t, in_s, col_t, col_s, row_t, row_s, t_sc, s_sc, acc,
+    row_stat, col_stat, col_part, div_in, wide, col_level, w_row, q_tr, w_high, w_low,
+    part, x_in, x_sum, y_in, turned, turned_in, total_in,
+    load_sem, slot_sem, x_send, x_recv, z_send, z_recv,
+    row_send, row_recv, end_send, end_recv, col_send, col_recv, div_send, div_recv,
+    px_send, px_recv, py_send, py_recv, pz_send, pz_recv, out_send, out_recv, total_send, total_recv,
+):
+    chunks = rows // CHUNK
+    pb = lax.axis_index("pb")
+    ka = lax.axis_index("ka")
+    seq = pb % batches
+    y = pb // batches
+    z = ka // 2
+    x = ka % 2
+    place = x * groups + y
+    low = jnp.where(seq == 0, y, groups - 1 - y)
+    high = levels - 1 - low
+    sources = (low, high)
+    outer = low == 0
+    inner_level = jnp.logical_and(z > 0, z < levels - 1)
+    end_level = jnp.logical_not(inner_level)
+    active = jnp.logical_or(outer, inner_level)
+    turning = jnp.logical_and(outer, inner_level)
+    outer_end = jnp.logical_and(outer, end_level)
+    y_outer = seq
+    y_inner = 1 - seq
+    mate = y * batches + (1 - seq)
+    x_device = (pb, z * 2 + (1 - x))
+
+    planes = []
+    for step in range(1, 2 * groups):
+        other = (place + step) % (2 * groups)
+        planes.append(((other % groups) * batches + seq, z * 2 + other // groups))
+    line = [(pb, ((z + step) % levels) * 2 + x) for step in range(1, levels)]
+    barrier = pltpu.get_barrier_semaphore()
+    count = 2 * groups * levels
+    index = place * levels + z
+
+    def greet(step, carry):
+        other = (index + step) % count
+        spot, level = other // levels, other % levels
+        device = ((spot % groups) * batches + seq, level * 2 + spot // groups)
+        pl.semaphore_signal(barrier, inc=1, device_id=device, device_id_type=MESH)
+        return carry
+
+    lax.fori_loop(1, count, greet, 0)
+    diagonal = (1 - y) * batches + (1 - seq)
+    for other in (mate, diagonal):
+        pl.semaphore_signal(barrier, inc=1, device_id=(other, ka), device_id_type=MESH)
+
+    loads = [
+        pltpu.make_async_copy(t_hbm.at[seq], in_t.at[0], load_sem.at[0]),
+        pltpu.make_async_copy(s_hbm.at[seq], in_s.at[0], load_sem.at[1]),
+    ]
+    for slot in range(2):
+        @pl.when(z == sources[slot])
+        def _():
+            pltpu.make_async_copy(t_hbm.at[seq], col_t.at[slot], slot_sem.at[slot, 0]).start()
+            pltpu.make_async_copy(s_hbm.at[seq], col_s.at[slot], slot_sem.at[slot, 1]).start()
+    for load in loads:
+        load.start()
+    pl.semaphore_wait(barrier, count + 1)
+
+    x_copies = [
+        pltpu.make_async_remote_copy(
+            src_ref=src.at[seq], dst_ref=dst, send_sem=x_send.at[i], recv_sem=x_recv.at[i],
+            device_id=x_device, device_id_type=MESH,
+        )
+        for i, (src, dst) in enumerate(((t_hbm, in_t.at[1]), (s_hbm, in_s.at[1])))
+    ]
+
+    def z_copies(slot, j, to):
+        span = pl.ds(pl.multiple_of(j * CHUNK, CHUNK), CHUNK)
+        return [
+            pltpu.make_async_remote_copy(
+                src_ref=buf.at[slot, span, :], dst_ref=buf.at[slot, span, :],
+                send_sem=z_send.at[to, slot, j, i], recv_sem=z_recv.at[slot, j, i],
+                device_id=(pb, to * 2 + x), device_id_type=MESH,
+            )
+            for i, buf in enumerate((col_t, col_s))
+        ]
+
+    for slot in range(2):
+        @pl.when(z == sources[slot])
+        def _():
+            pltpu.make_async_copy(t_hbm.at[seq], col_t.at[slot], slot_sem.at[slot, 0]).wait()
+            pltpu.make_async_copy(s_hbm.at[seq], col_s.at[slot], slot_sem.at[slot, 1]).wait()
+
+    last = levels - 1
+
+    def source_sends(slot, to):
+        return jnp.logical_and(z == sources[slot], to != z) if 0 < to < last else None
+
+    def forwards(slot, to):
+        beside = 1 if to == 0 else last - 1
+        return jnp.logical_and(jnp.logical_and(outer, z == beside), sources[slot] != to)
+
+    def put_rows(xb, teacher, student):
+        t_high, t_low = split((teacher * (LOG2E / math.sqrt(DT))).T)
+        s_high, s_low = split((student * (LOG2E / math.sqrt(DS))).T)
+        for part_index, (t_part, s_part) in enumerate(
+            ((t_high, s_high), (t_low, s_low), (t_high, s_high))
+        ):
+            row_t[xb, part_index * DT:(part_index + 1) * DT, :] = t_part
+            row_s[xb, part_index * DS:(part_index + 1) * DS, :] = s_part
+
+    def relate(xb, j):
+        span = pl.ds(pl.multiple_of(j * CHUNK, CHUNK), CHUNK)
+        t_high, t_low = split(col_t[:, span, :].reshape(2 * CHUNK, DT))
+        s_high, s_low = split(col_s[:, span, :].reshape(2 * CHUNK, DS))
+        teacher = nn(jnp.concatenate([t_high, t_high, t_low], axis=1), row_t[xb])
+        student = nn(jnp.concatenate([s_high, s_high, s_low], axis=1), row_s[xb])
+        tiles = []
+        for slot in range(2):
+            base = slot * rows + j * CHUNK
+            at = pl.ds(pl.multiple_of(base, CHUNK), CHUNK)
+            t_sc[xb, at, :] = teacher[slot * CHUNK:(slot + 1) * CHUNK]
+            s_sc[xb, at, :] = student[slot * CHUNK:(slot + 1) * CHUNK]
+            tiles += [pl.ds(pl.multiple_of(base + i * PART, PART), PART) for i in range(CHUNK // PART)]
+
+        def read(ref, at):
+            return ref[xb, at, :].reshape(PART // 8, 8, rows)
+
+        t_old, s_old = acc[xb, 0], acc[xb, 3]
+        t_max, s_max = t_old, s_old
+        for at in tiles:
+            t_max = jnp.maximum(t_max, jnp.max(read(t_sc, at), axis=0))
+            s_max = jnp.maximum(s_max, jnp.max(read(s_sc, at), axis=0))
+        t_scale = jnp.exp2(t_old - t_max)
+        s_scale = jnp.exp2(s_old - s_max)
+        t_sum, cross, s_sum = acc[xb, 1] * t_scale, acc[xb, 2] * t_scale, acc[xb, 4] * s_scale
+        for at in tiles:
+            t_tile, s_tile = read(t_sc, at), read(s_sc, at)
+            t_exp = jnp.exp2(t_tile - t_max[None])
+            t_sum = t_sum + jnp.sum(t_exp, axis=0)
+            cross = cross + jnp.sum(t_exp * (t_tile - s_tile), axis=0)
+            s_sum = s_sum + jnp.sum(jnp.exp2(s_tile - s_max[None]), axis=0)
+        acc[xb, 0] = t_max
+        acc[xb, 1] = t_sum
+        acc[xb, 2] = cross
+        acc[xb, 3] = s_max
+        acc[xb, 4] = s_sum
+
+    def turn(j):
+        for slot in range(2):
+            at = pl.ds(pl.multiple_of(slot * rows + j * CHUNK, PART), CHUNK)
+            t_top = jnp.max(jnp.maximum(t_sc[0, at, :], t_sc[1, at, :]), axis=1, keepdims=True)
+            s_top = jnp.max(jnp.maximum(s_sc[0, at, :], s_sc[1, at, :]), axis=1, keepdims=True)
+            t_all = c_all = s_all = jnp.zeros((CHUNK, rows), jnp.float32)
+            for xb in range(2):
+                t_exp = jnp.exp2(t_sc[xb, at, :] - t_top)
+                t_all = t_all + t_exp
+                c_all = c_all + t_exp * (t_sc[xb, at, :] - s_sc[xb, at, :])
+                s_all = s_all + jnp.exp2(s_sc[xb, at, :] - s_top)
+            sums = [jnp.sum(v, axis=1, keepdims=True) for v in (t_all, c_all, s_all)]
+            col_part[at, 0:1] = t_top
+            col_part[at, 1:2] = sums[0]
+            col_part[at, 2:3] = sums[1]
+            col_part[at, 3:4] = s_top
+            col_part[at, 4:5] = sums[2]
+            col_part[at, 5:8] = jnp.zeros((CHUNK, 3), jnp.float32)
+
+    for xb in range(2):
+        for kind in range(5):
+            start = -jnp.inf if kind in (0, 3) else 0.0
+            acc[xb, kind] = jnp.full((8, rows), start, jnp.float32)
+
+    @pl.when(active)
+    def _():
+        for copy in x_copies:
+            copy.start()
+
+
+    def first_send(j, carry):
+        for slot in range(2):
+            for to in range(1, last):
+                @pl.when(source_sends(slot, to))
+                def _():
+                    for copy in z_copies(slot, j, to):
+                        copy.start()
+        return carry
+
+    lax.fori_loop(0, chunks, first_send, 0)
+    half = chunks // 2
+
+    def arrive(j):
+        for slot in range(2):
+            @pl.when(z != sources[slot])
+            def _():
+                for copy in z_copies(slot, j, 1):
+                    copy.wait_recv()
+                for to in (0, last):
+                    @pl.when(forwards(slot, to))
+                    def _():
+                        for copy in z_copies(slot, j, to):
+                            copy.start()
+
+    def gather(k, carry):
+        late = k - half
+        phase = jnp.where(k < half, 1, late % 3)
+        j = jnp.where(k < half, k, late // 3 + jnp.where(phase == 0, 0, half))
+        own = phase == 1
+
+        @pl.when(k == half)
+        def _():
+            for copy in x_copies:
+                copy.wait_recv()
+
+        @pl.when(jnp.logical_or(k == 0, k == half))
+        def _():
+            which = jnp.where(k == 0, 0, 1)
+            put_rows(jnp.where(k == 0, x, 1 - x), in_t[which], in_s[which])
+
+        @pl.when(own)
+        def _():
+            arrive(j)
+
+        relate(jnp.where(own, x, 1 - x), j)
+
+        @pl.when(jnp.logical_and(turning, jnp.logical_not(own)))
+        def _():
+            turn(j)
+        return carry
+
+    for load in loads:
+        load.wait()
+    lax.fori_loop(0, jnp.where(active, 2 * chunks, 0), gather, 0)
+
+    mine = jnp.where(inner_level, place, x)
+
+    @pl.when(active)
+    def _():
+        for xb in range(2):
+            t_max, s_max = acc[xb, 0], acc[xb, 3]
+            t_top = jnp.max(t_max, axis=0, keepdims=True)
+            s_top = jnp.max(s_max, axis=0, keepdims=True)
+            t_scale = jnp.exp2(t_max - t_top)
+            s_scale = jnp.exp2(s_max - s_top)
+            t_sum = jnp.sum(acc[xb, 1] * t_scale, axis=0, keepdims=True)
+            cross = jnp.sum(acc[xb, 2] * t_scale, axis=0, keepdims=True)
+            s_sum = jnp.sum(acc[xb, 4] * s_scale, axis=0, keepdims=True)
+            row_stat[mine, xb] = jnp.concatenate(
+                [t_top, t_sum, cross, s_top, s_sum, jnp.zeros((3, rows), jnp.float32)], axis=0
+            )
+
+    @pl.when(turning)
+    def _():
+        for slot in range(2):
+            col_stat[slot, 1 + z] = col_part[slot * rows:(slot + 1) * rows, :].T
+
+    def remote(src, dst, send, recv, device):
+        return pltpu.make_async_remote_copy(
+            src_ref=src, dst_ref=dst, send_sem=send, recv_sem=recv,
+            device_id=device, device_id_type=MESH,
+        )
+
+    outer_pb = y_outer * batches + seq
+    inner_pb = y_inner * batches + seq
+    other_inner = last - z
+    my_slot = jnp.where(z * 2 < levels, 0, 1)
+
+    def inner_sends():
+        copies = [
+            remote(row_stat.at[place], row_stat.at[place], row_send.at[step], row_recv.at[place], planes[step - 1])
+            for step in range(1, 2 * groups)
+        ]
+        for xb in range(2):
+            copies.append(remote(
+                row_stat.at[place, xb], col_stat.at[my_slot, place], col_send.at[xb, 0],
+                col_recv.at[my_slot, place], (inner_pb, other_inner * 2 + xb),
+            ))
+        return copies
+
+    def turning_sends():
+        copies = []
+        for slot, end in ((0, 0), (1, last)):
+            src = col_stat.at[slot, 1 + z]
+            for xb in range(2):
+                copies.append(remote(
+                    src, row_stat.at[1 + z, x], end_send.at[slot, xb], end_recv.at[z - 1, x],
+                    (pb, end * 2 + xb),
+                ))
+            for i, level in enumerate((other_inner, last - end)):
+                copies.append(remote(
+                    src, col_stat.at[slot, 1 + z], end_send.at[slot, 2 + i], col_recv.at[slot, 1 + z],
+                    (pb, level * 2 + x),
+                ))
+        return copies
+
+    def end_sends():
+        copies = [remote(row_stat.at[x], row_stat.at[x], row_send.at[0], row_recv.at[x], x_device)]
+        for xb in range(2):
+            for i, level in enumerate((1, last - 1, last - z)):
+                copies.append(remote(
+                    row_stat.at[x, xb], col_stat.at[my_slot, x], col_send.at[xb, 1 + i],
+                    col_recv.at[my_slot, x], (pb, level * 2 + xb),
+                ))
+        return copies
+
+    kinds = ((turning, turning_sends), (inner_level, inner_sends), (outer_end, end_sends))
+    for case, sends in kinds:
+        @pl.when(case)
+        def _():
+            for copy in sends():
+                copy.start()
+
+    @pl.when(active)
+    def _():
+        for slot in range(2):
+            high_part, low_part = split((col_s[slot] * (1.0 / math.sqrt(DS))).T)
+            q_tr[0:DS, slot * rows:(slot + 1) * rows] = high_part
+            q_tr[DS:2 * DS, slot * rows:(slot + 1) * rows] = low_part
+
+    def landed(ref, sem):
+        remote(ref, ref, row_send.at[0], sem, x_device).wait_recv()
+
+    @pl.when(inner_level)
+    def _():
+        for step in range(1, 2 * groups):
+            other = (place + step) % (2 * groups)
+            landed(row_stat.at[other], row_recv.at[other])
+
+    @pl.when(outer_end)
+    def _():
+        landed(row_stat.at[1 - x], row_recv.at[1 - x])
+        for xb in range(2):
+            for level in range(2):
+                landed(row_stat.at[2 + level, xb], end_recv.at[level, xb])
+
+    def combine(stats):
+        t_max = functools.reduce(jnp.maximum, [stat[0:1] for stat in stats])
+        s_max = functools.reduce(jnp.maximum, [stat[3:4] for stat in stats])
+        t_sum = cross = s_sum = jnp.zeros((1, rows), jnp.float32)
+        for stat in stats:
+            t_scale = jnp.exp2(stat[0:1] - t_max)
+            t_sum = t_sum + stat[1:2] * t_scale
+            cross = cross + stat[2:3] * t_scale
+            s_sum = s_sum + stat[4:5] * jnp.exp2(stat[3:4] - s_max)
+        t_level = t_max + jnp.log2(t_sum)
+        s_level = s_max + jnp.log2(s_sum)
+        return t_level, s_level, LN2 * (cross / t_sum - t_level + s_level)
+
+    @pl.when(active)
+    def _():
+        divergence = jnp.zeros((1, rows), jnp.float32)
+        for xb in range(2):
+            t_level, s_level, share = combine([row_stat[other, xb] for other in range(2 * groups)])
+            wide[xb] = jnp.concatenate([t_level, s_level], axis=0)
+            divergence = divergence + share
+        div_in[z] = jnp.broadcast_to(divergence, (8, rows))
+
+    def div_copy(step, slot):
+        return pltpu.make_async_remote_copy(
+            src_ref=div_in.at[slot], dst_ref=div_in.at[slot],
+            send_sem=div_send.at[step], recv_sem=div_recv.at[step],
+            device_id=line[step - 1], device_id_type=MESH,
+        )
+
+    @pl.when(outer)
+    def _():
+        for step in range(1, levels):
+            div_copy(step, z).start()
+
+    tiles = 2 * rows // TILE
+
+    def row_weights(xb):
+        rows_t = wide[xb, 0:1, :]
+        rows_s = wide[xb, 1:2, :]
+
+        def tile(j, carry):
+            at = pl.ds(pl.multiple_of(j * TILE, TILE), TILE)
+            w_row[xb, at, :] = jnp.exp2(s_sc[xb, at, :] - rows_s) - jnp.exp2(t_sc[xb, at, :] - rows_t)
+            return carry
+
+        lax.fori_loop(0, tiles, tile, 0)
+
+    def both_weights(xb, carry):
+        row_weights(xb)
+        return carry
+
+    passes = jnp.where(active, 2, 0)
+    lax.fori_loop(0, passes, both_weights, 0)
+    for slot in range(2):
+        @pl.when(jnp.logical_and(active, z == sources[slot]))
+        def _():
+            for other in range(2 * groups):
+                col_stat[slot, other] = row_stat[other, x]
+
+        @pl.when(jnp.logical_and(active, z != sources[slot]))
+        def _():
+            for other in range(2 * groups):
+                @pl.when(jnp.logical_not(jnp.logical_and(turning, other == 1 + z)))
+                def _():
+                    landed(col_stat.at[slot, other], col_recv.at[slot, other])
+
+    @pl.when(active)
+    def _():
+        for slot in range(2):
+            t_level, s_level, _ = combine([col_stat[slot, other] for other in range(2 * groups)])
+            both = jnp.concatenate([t_level, s_level, jnp.zeros((6, rows), jnp.float32)], axis=0)
+            col_level[slot * rows:(slot + 1) * rows, :] = both.T
+
+    blocks = rows // LANES
+
+    def px_copy(b):
+        return pltpu.make_async_remote_copy(
+            src_ref=part.at[1 - x, b], dst_ref=x_in.at[b],
+            send_sem=px_send.at[b], recv_sem=px_recv.at[b],
+            device_id=x_device, device_id_type=MESH,
+        )
+
+    def py_copy(step, b):
+        return pltpu.make_async_remote_copy(
+            src_ref=x_sum.at[b], dst_ref=y_in.at[step, b],
+            send_sem=py_send.at[step, b], recv_sem=py_recv.at[step, b],
+            device_id=(((y + step) % groups) * batches + seq, ka), device_id_type=MESH,
+        )
+
+    def out_copy(which, b):
+        span = pl.ds(b * LANES, LANES)
+        return pltpu.make_async_remote_copy(
+            src_ref=out_ref.at[which, span, :], dst_ref=out_ref.at[which, span, :],
+            send_sem=out_send.at[b], recv_sem=out_recv.at[b],
+            device_id=(mate, ka), device_id_type=MESH,
+        )
+
+    totals = [(((1 - y) * batches + seq), ka), (mate, ka), (diagonal, ka)]
+
+    def total_copy(i):
+        return remote(total_in.at[seq], total_in.at[seq], total_send.at[i], total_recv.at[seq], totals[i])
+
+    def turned_copy(slot, b):
+        end = 0 if slot == 0 else last
+        return remote(
+            turned.at[slot, b], turned_in.at[z - 1, b], pz_send.at[slot, b], pz_recv.at[z - 1, b],
+            (pb, end * 2 + x),
+        )
+
+    def gradient(xb):
+        def tile(j, carry):
+            at = pl.ds(pl.multiple_of(j * TILE, TILE), TILE)
+            col = col_level[at, :]
+            weight = (
+                w_row[xb, at, :]
+                + jnp.exp2(s_sc[xb, at, :] - col[:, 1:2])
+                - jnp.exp2(t_sc[xb, at, :] - col[:, 0:1])
+            )
+            high_part, low_part = split(weight)
+            w_high[at, :] = high_part
+            w_low[at, :] = low_part
+            return carry
+
+        lax.fori_loop(0, tiles, tile, 0)
+        first = nn(q_tr[...], w_high[...])
+        product = first[:DS] + first[DS:] + nn(q_tr[0:DS, :], w_low[...])
+        for b in range(blocks):
+            part[xb, b] = product[:, b * LANES:(b + 1) * LANES]
+
+        @pl.when(turning)
+        def _():
+            q_rows = row_s[xb, 0:2 * DS, :]
+            back = nt(q_rows, w_high[...])
+            back = (back[:DS] + back[DS:] + nt(q_rows[:DS], w_low[...])) * LN2
+            for slot in range(2):
+                for b in range(blocks):
+                    piece = back[:, slot * rows + b * LANES:slot * rows + (b + 1) * LANES]
+                    turned[slot, b] = jnp.where(xb == x, turned[slot, b] + piece, piece)
+
+    def both_gradients(step, carry):
+        gradient(jnp.where(step == 0, 1 - x, x))
+
+        @pl.when(step == 0)
+        def _():
+            for b in range(blocks):
+                px_copy(b).start()
+        return carry
+
+    lax.fori_loop(0, passes, both_gradients, 0)
+
+    @pl.when(turning)
+    def _():
+        for b in range(blocks):
+            for slot in range(2):
+                turned_copy(slot, b).start()
+
+    sends_y = jnp.logical_or(inner_level, outer)
+    gets_y = jnp.logical_or(inner_level, jnp.logical_not(outer))
+    for b in range(blocks):
+        @pl.when(active)
+        def _():
+            px_copy(b).wait_recv()
+            x_sum[b] = part[x, b] + x_in[b]
+
+        @pl.when(outer_end)
+        def _():
+            for level in range(2):
+                landed(turned_in.at[level, b], pz_recv.at[level, b])
+                x_sum[b] = x_sum[b] + turned_in[level, b]
+
+        @pl.when(sends_y)
+        def _():
+            py_copy(1, b).start()
+
+    @pl.when(outer)
+    def _():
+        for step in range(1, levels):
+            div_copy(step, (z - step + levels) % levels).wait_recv()
+        total = div_in[0, 0:1, :]
+        for level in range(1, levels):
+            total = total + div_in[level, 0:1, :]
+        total_in[seq] = jnp.broadcast_to(total, (8, rows))
+        for i in range(3):
+            total_copy(i).start()
+
+    for b in range(blocks):
+        span = slice(b * LANES, (b + 1) * LANES)
+
+        @pl.when(gets_y)
+        def _():
+            py_copy(1, b).wait_recv()
+
+        @pl.when(inner_level)
+        def _():
+            out_ref[seq, span, :] = (x_sum[b] + y_in[1, b]).T
+
+        @pl.when(outer_end)
+        def _():
+            out_ref[seq, span, :] = x_sum[b].T
+
+        @pl.when(jnp.logical_not(active))
+        def _():
+            out_ref[seq, span, :] = y_in[1, b].T
+        out_copy(seq, b).start()
+
+    landed(total_in.at[1 - seq], total_recv.at[1 - seq])
+
+    @pl.when(jnp.logical_not(outer))
+    def _():
+        landed(total_in.at[seq], total_recv.at[seq])
+    loss_ref[0, 0] = jnp.sum(total_in[0, 0:1, :] + total_in[1, 0:1, :]) / (
+        batches * HEADS * rows * 2 * levels
+    )
+
+    @pl.when(outer)
+    def _():
+        for i in range(3):
+            total_copy(i).wait_send()
+
+    @pl.when(active)
+    def _():
+        for copy in x_copies:
+            copy.wait_send()
+
+    def sent(j, carry):
+        for slot in range(2):
+            for to in range(levels):
+                goes = source_sends(slot, to) if 0 < to < last else forwards(slot, to)
+
+                @pl.when(goes)
+                def _():
+                    for copy in z_copies(slot, j, to):
+                        copy.wait_send()
+        return carry
+
+    lax.fori_loop(0, chunks, sent, 0)
+    for case, sends in kinds:
+        @pl.when(case)
+        def _():
+            for copy in sends():
+                copy.wait_send()
+
+    @pl.when(outer)
+    def _():
+        for step in range(1, levels):
+            div_copy(step, z).wait_send()
+
+    for b in range(blocks):
+        @pl.when(active)
+        def _():
+            px_copy(b).wait_send()
+
+        @pl.when(turning)
+        def _():
+            for slot in range(2):
+                turned_copy(slot, b).wait_send()
+
+        @pl.when(sends_y)
+        def _():
+            py_copy(1, b).wait_send()
+        out_copy(seq, b).wait_send()
+        out_copy(1 - seq, b).wait_recv()
+
+
 def solution(mesh):
     def shards(teacher_q, student_q):
         batches, rows = teacher_q.shape[0], teacher_q.shape[1]
@@ -474,8 +1076,99 @@
         blocks = rows // LANES
         f32, bf16 = jnp.float32, jnp.bfloat16
         dma = pltpu.SemaphoreType.DMA
+        folds = groups == 2 and levels == 4
+        chosen = folded_kernel if folds else kernel
+        scratch = [
+            pltpu.VMEM((2, rows, DT), f32),
+            pltpu.VMEM((2, rows, DS), f32),
+            pltpu.VMEM((2, rows, DT), f32),
+            pltpu.VMEM((2, rows, DS), f32),
+            pltpu.VMEM((2, 3 * DT, rows), bf16),
+            pltpu.VMEM((2, 3 * DS, rows), bf16),
+            pltpu.VMEM((2, 2 * rows, rows), f32),
+            pltpu.VMEM((2, 2 * rows, rows), f32),
+            pltpu.VMEM((2, 5, 8, rows), f32),
+        ]
+        scratch += [
+            pltpu.VMEM((4, 2, 8, rows), f32),
+            pltpu.VMEM((2, 4, 8, rows), f32),
+            pltpu.VMEM((2 * rows, 8), f32),
+            pltpu.VMEM((levels, 8, rows), f32),
+            pltpu.VMEM((2, 2, rows), f32),
+            pltpu.VMEM((2 * rows, 8), f32),
+            pltpu.VMEM((2, 2 * rows, rows), f32),
+            pltpu.VMEM((2 * DS, 2 * rows), bf16),
+            pltpu.VMEM((2 * rows, rows), bf16),
+            pltpu.VMEM((2 * rows, rows), bf16),
+            pltpu.VMEM((2, blocks, DS, LANES), f32),
+            pltpu.VMEM((blocks, DS, LANES), f32),
+            pltpu.VMEM((blocks, DS, LANES), f32),
+            pltpu.VMEM((groups, blocks, DS, LANES), f32),
+            pltpu.VMEM((2, blocks, DS, LANES), f32),
+            pltpu.VMEM((2, blocks, DS, LANES), f32),
+            pltpu.VMEM((batches, 8, rows), f32),
+            dma((2,)),
+            dma((2, 2)),
+            dma((2,)),
+            dma((2,)),
+            dma((levels, 2, chunks, 2)),
+            dma((2, chunks, 2)),
+            dma((4,)),
+            dma((4,)),
+            dma((2, 4)),
+            dma((2, 2)),
+            dma((2, 4)),
+            dma((2, 4)),
+            dma((levels,)),
+            dma((levels,)),
+            dma((blocks,)),
+            dma((blocks,)),
+            dma((groups, blocks)),
+            dma((groups, blocks)),
+            dma((2, blocks)),
+            dma((2, blocks)),
+            dma((blocks,)),
+            dma((blocks,)),
+            dma((3,)),
+            dma((2,)),
+        ] if folds else [
+            pltpu.VMEM((2 * groups, 2, 8, rows), f32),
+            pltpu.VMEM((2, 2 * groups, 8, rows), f32),
+            pltpu.VMEM((levels, 8, rows), f32),
+            pltpu.VMEM((2, 2, rows), f32),
+            pltpu.VMEM((2 * rows, 8), f32),
+            pltpu.VMEM((2, 2 * rows, rows), f32),
+            pltpu.VMEM((2 * DS, 2 * rows), bf16),
+            pltpu.VMEM((2 * rows, rows), bf16),
+            pltpu.VMEM((2 * rows, rows), bf16),
+            pltpu.VMEM((2, blocks, DS, LANES), f32),
+            pltpu.VMEM((blocks, DS, LANES), f32),
+            pltpu.VMEM((blocks, DS, LANES), f32),
+            pltpu.VMEM((groups, blocks, DS, LANES), f32),
+            pltpu.VMEM((batches, 8, rows), f32),
+            dma((2,)),
+            dma((2, 2)),
+            dma((2,)),
+            dma((2,)),
+            dma((levels, 2, chunks, 2)),
+            dma((2, chunks, 2)),
+            dma((2 * groups,)),
+            dma((2 * groups,)),
+            dma((2, levels)),
+            dma((2, 2 * groups)),
+            dma((levels,)),
+            dma((levels,)),
+            dma((blocks,)),
+            dma((blocks,)),
+            dma((groups, blocks)),
+            dma((groups, blocks)),
+            dma((blocks,)),
+            dma((blocks,)),
+            dma,
+            dma,
+        ]
         grad, loss = pl.pallas_call(
-            functools.partial(kernel, groups, levels, rows, batches),
+            functools.partial(chosen, groups, levels, rows, batches),
             out_shape=(
                 jax.ShapeDtypeStruct((batches, rows, DS), f32),
                 jax.ShapeDtypeStruct((1, 1), f32),
@@ -485,53 +1178,9 @@
                 pl.BlockSpec(memory_space=pltpu.VMEM),
                 pl.BlockSpec(memory_space=pltpu.SMEM),
             ),
-            scratch_shapes=[
-                pltpu.VMEM((2, rows, DT), f32),
-                pltpu.VMEM((2, rows, DS), f32),
-                pltpu.VMEM((2, rows, DT), f32),
-                pltpu.VMEM((2, rows, DS), f32),
-                pltpu.VMEM((2, 3 * DT, rows), bf16),
-                pltpu.VMEM((2, 3 * DS, rows), bf16),
-                pltpu.VMEM((2, 2 * rows, rows), f32),
-                pltpu.VMEM((2, 2 * rows, rows), f32),
-                pltpu.VMEM((2, 5, 8, rows), f32),
-                pltpu.VMEM((2 * groups, 2, 8, rows), f32),
-                pltpu.VMEM((2, 2 * groups, 8, rows), f32),
-                pltpu.VMEM((levels, 8, rows), f32),
-                pltpu.VMEM((2, 2, rows), f32),
-                pltpu.VMEM((2 * rows, 8), f32),
-                pltpu.VMEM((2, 2 * rows, rows), f32),
-                pltpu.VMEM((2 * DS, 2 * rows), bf16),
-                pltpu.VMEM((2 * rows, rows), bf16),
-                pltpu.VMEM((2 * rows, rows), bf16),
-                pltpu.VMEM((2, blocks, DS, LANES), f32),
-                pltpu.VMEM((blocks, DS, LANES), f32),
-                pltpu.VMEM((blocks, DS, LANES), f32),
-                pltpu.VMEM((groups, blocks, DS, LANES), f32),
-                pltpu.VMEM((batches, 8, rows), f32),
-                dma((2,)),
-                dma((2, 2)),
-                dma((2,)),
-                dma((2,)),
-                dma((levels, 2, chunks, 2)),
-                dma((2, chunks, 2)),
-                dma((2 * groups,)),
-                dma((2 * groups,)),
-                dma((2, levels)),
-                dma((2, 2 * groups)),
-                dma((levels,)),
-                dma((levels,)),
-                dma((blocks,)),
-                dma((blocks,)),
-                dma((groups, blocks)),
-                dma((groups, blocks)),
-                dma((blocks,)),
-                dma((blocks,)),
-                dma,
-                dma,
-            ],
+            scratch_shapes=scratch,
             compiler_params=pltpu.CompilerParams(
-                collective_id=0, has_side_effects=True, vmem_limit_bytes=60 * 1024 * 1024
+                collective_id=1 if folds else 0, has_side_effects=True, vmem_limit_bytes=60 * 1024 * 1024
             ),
         )(teacher_q, student_q)
         return grad, loss.reshape(())

time: 52.8 us -> 54.2 us (1.027)
  Pallas kernels: 48.5 us -> 49.3 us
    pallas_call x1, Pallas kernels: 48.5 us -> 49.3 us  [shards(): pl.pallas_call(functools.partial(chosen, groups, levels, rows, batches),...]
where the time goes in v6:
time: 54.2 us; the launch traced here: 53.5 us
  Pallas kernels  49.3 us (91%)
  between operations  2.39 us (4%)
  local copies, waits for them, and re-layouts  1.77 us (3%)
    pallas_call x1, Pallas kernels, shards(): pl.pallas_call(functools.partial(chosen, groups, levels, rows, batches),...  49.3 us
    unnamed x1, local copies, waits for them, and re-layouts  1.77 us

profile of v6, /device:TPU:0, one launch (start us, length us, event | category | flops | bytes accessed | tf_op | source)
XLA Modules:
  0.0 53.5 jit_solution(15383086365695865659)
XLA Ops:
  0.6 49.3 %shard_map.41 = (f32[2,384,128]{2,1,0:T(8,128)}, f32[1,1]{1,0:T(1,128)}) custom-call(f32[2,384,256]{2,1,0:T(8,128)} %t_hbm.1, f32[2,384,128]{2,1,0:T(8,128)} %s_hbm.1), custom_call_target="tpu_custom_call" | custom-call | tf_op jit(solution)/shard_map/pallas_call | solution.py:1170
  50.0 1.8 %copy.6 = f32[2,384,128]{2,1,0:T(8,128)} copy(f32[2,384,128]{2,1,0:T(8,128)} %get-tuple-element.8) | data formatting | bytes 786432

commit v7 on v6

--- a/solution.py
+++ b/solution.py
@@ -24,12 +24,6 @@
     high = values.astype(jnp.bfloat16)
     low = (values - high.astype(jnp.float32)).astype(jnp.bfloat16)
     return high, low
-
-
-def nt(left, right):
-    return lax.dot_general(
-        left, right, (((1,), (1,)), ((), ())), preferred_element_type=jnp.float32
-    )
 
 
 def nn(left, right):
@@ -474,7 +468,7 @@
 def folded_kernel(
     groups, levels, rows, batches,
     t_hbm, s_hbm, out_ref, loss_ref,
-    in_t, in_s, col_t, col_s, row_t, row_s, t_sc, s_sc, acc,
+    in_t, in_s, row_n, col_t, col_s, row_t, row_s, t_sc, s_sc, acc,
     row_stat, col_stat, col_part, div_in, wide, col_level, w_row, q_tr, w_high, w_low,
     part, x_in, x_sum, y_in, turned, turned_in, total_in,
     load_sem, slot_sem, x_send, x_recv, z_send, z_recv,
@@ -537,13 +531,18 @@
         load.start()
     pl.semaphore_wait(barrier, count + 1)
 
-    x_copies = [
-        pltpu.make_async_remote_copy(
-            src_ref=src.at[seq], dst_ref=dst, send_sem=x_send.at[i], recv_sem=x_recv.at[i],
-            device_id=x_device, device_id_type=MESH,
-        )
-        for i, (src, dst) in enumerate(((t_hbm, in_t.at[1]), (s_hbm, in_s.at[1])))
-    ]
+    y_device = ((1 - y) * batches + seq, ka)
+
+    def piece_copies(q, over_x):
+        span = pl.ds(pl.multiple_of(q * CHUNK, CHUNK), CHUNK)
+        return [
+            pltpu.make_async_remote_copy(
+                src_ref=src.at[seq, span, :] if over_x else dst.at[1, span, :], dst_ref=dst.at[1, span, :],
+                send_sem=x_send.at[0 if over_x else 1, q, i], recv_sem=x_recv.at[q, i],
+                device_id=x_device if over_x else y_device, device_id_type=MESH,
+            )
+            for i, (src, dst) in enumerate(((t_hbm, in_t), (s_hbm, in_s)))
+        ]
 
     def z_copies(slot, j, to):
         span = pl.ds(pl.multiple_of(j * CHUNK, CHUNK), CHUNK)
@@ -574,6 +573,7 @@
     def put_rows(xb, teacher, student):
         t_high, t_low = split((teacher * (LOG2E / math.sqrt(DT))).T)
         s_high, s_low = split((student * (LOG2E / math.sqrt(DS))).T)
+        row_n[xb] = jnp.concatenate(split(student * (1.0 / math.sqrt(DS))), axis=1)
         for part_index, (t_part, s_part) in enumerate(
             ((t_high, s_high), (t_low, s_low), (t_high, s_high))
         ):
@@ -641,10 +641,15 @@
             start = -jnp.inf if kind in (0, 3) else 0.0
             acc[xb, kind] = jnp.full((8, rows), start, jnp.float32)
 
+    half = chunks // 2
+
     @pl.when(active)
     def _():
-        for copy in x_copies:
-            copy.start()
+        for q in range(chunks):
+            @pl.when(jnp.logical_or(end_level, q // half == y))
+            def _():
+                for copy in piece_copies(q, True):
+                    copy.start()
 
 
     def first_send(j, carry):
@@ -657,8 +662,6 @@
         return carry
 
     lax.fori_loop(0, chunks, first_send, 0)
-    half = chunks // 2
-
     def arrive(j):
         for slot in range(2):
             @pl.when(z != sources[slot])
@@ -679,8 +682,11 @@
 
         @pl.when(k == half)
         def _():
-            for copy in x_copies:
-                copy.wait_recv()
+            for q in range(chunks):
+                @pl.when(jnp.logical_or(end_level, q // half != y))
+                def _():
+                    for copy in piece_copies(q, True):
+                        copy.wait_recv()
 
         @pl.when(jnp.logical_or(k == 0, k == half))
         def _():
@@ -690,6 +696,13 @@
         @pl.when(own)
         def _():
             arrive(j)
+
+        @pl.when(jnp.logical_and(inner_level, k < half))
+        def _():
+            for copy in piece_copies(y * half + k, True):
+                copy.wait_recv()
+            for copy in piece_copies(y * half + k, False):
+                copy.start()
 
         relate(jnp.where(own, x, 1 - x), j)
 
@@ -932,23 +945,27 @@
         for b in range(blocks):
             part[xb, b] = product[:, b * LANES:(b + 1) * LANES]
 
-        @pl.when(turning)
-        def _():
-            q_rows = row_s[xb, 0:2 * DS, :]
-            back = nt(q_rows, w_high[...])
-            back = (back[:DS] + back[DS:] + nt(q_rows[:DS], w_low[...])) * LN2
-            for slot in range(2):
-                for b in range(blocks):
-                    piece = back[:, slot * rows + b * LANES:slot * rows + (b + 1) * LANES]
-                    turned[slot, b] = jnp.where(xb == x, turned[slot, b] + piece, piece)
+    def turn_back(xb):
+        back = nn(w_high[...], row_n[xb])
+        back = back[:, :DS] + back[:, DS:] + nn(w_low[...], row_n[xb, :, 0:DS])
+        for slot in range(2):
+            for b in range(blocks):
+                start = slot * rows + b * LANES
+                piece = back[start:start + LANES]
+                turned[slot, b] = jnp.where(xb == x, turned[slot, b] + piece, piece)
 
     def both_gradients(step, carry):
-        gradient(jnp.where(step == 0, 1 - x, x))
+        xb = jnp.where(step == 0, 1 - x, x)
+        gradient(xb)
 
         @pl.when(step == 0)
         def _():
             for b in range(blocks):
                 px_copy(b).start()
+
+        @pl.when(turning)
+        def _():
+            turn_back(xb)
         return carry
 
     lax.fori_loop(0, passes, both_gradients, 0)
@@ -971,7 +988,7 @@
         def _():
             for level in range(2):
                 landed(turned_in.at[level, b], pz_recv.at[level, b])
-                x_sum[b] = x_sum[b] + turned_in[level, b]
+            x_sum[b] = x_sum[b] + (turned_in[0, b] + turned_in[1, b]).T
 
         @pl.when(sends_y)
         def _():
@@ -1024,8 +1041,16 @@
 
     @pl.when(active)
     def _():
-        for copy in x_copies:
-            copy.wait_send()
+        for q in range(chunks):
+            @pl.when(jnp.logical_or(end_level, q // half == y))
+            def _():
+                for copy in piece_copies(q, True):
+                    copy.wait_send()
+
+            @pl.when(jnp.logical_and(inner_level, q // half == y))
+            def _():
+                for copy in piece_copies(q, False):
+                    copy.wait_send()
 
     def sent(j, carry):
         for slot in range(2):
@@ -1089,6 +1114,8 @@
             pltpu.VMEM((2, 2 * rows, rows), f32),
             pltpu.VMEM((2, 5, 8, rows), f32),
         ]
+        if folds:
+            scratch.insert(2, pltpu.VMEM((2, rows, 2 * DS), bf16))
         scratch += [
             pltpu.VMEM((4, 2, 8, rows), f32),
             pltpu.VMEM((2, 4, 8, rows), f32),
@@ -1104,13 +1131,13 @@
             pltpu.VMEM((blocks, DS, LANES), f32),
             pltpu.VMEM((blocks, DS, LANES), f32),
             pltpu.VMEM((groups, blocks, DS, LANES), f32),
-            pltpu.VMEM((2, blocks, DS, LANES), f32),
-            pltpu.VMEM((2, blocks, DS, LANES), f32),
+            pltpu.VMEM((2, blocks, LANES, DS), f32),
+            pltpu.VMEM((2, blocks, LANES, DS), f32),
             pltpu.VMEM((batches, 8, rows), f32),
             dma((2,)),
             dma((2, 2)),
-            dma((2,)),
-            dma((2,)),
+            dma((2, chunks, 2)),
+            dma((chunks, 2)),
             dma((levels, 2, chunks, 2)),
             dma((2, chunks, 2)),
             dma((4,)),
@@ -1180,9 +1207,9 @@
             ),
             scratch_shapes=scratch,
             compiler_params=pltpu.CompilerParams(
-                collective_id=1 if folds else 0, has_side_effects=True, vmem_limit_bytes=60 * 1024 * 1024
+                collective_id=1 if folds else 0, has_side_effects=True, vmem_limit_bytes=40 * 1024 * 1024
             ),
-        )(teacher_q, student_q)
+        )(pltpu.with_memory_space_constraint(teacher_q, pltpu.HBM), pltpu.with_memory_space_constraint(student_q, pltpu.HBM))
         return grad, loss.reshape(())
 
     in_specs = (P(None, "ka", None), P(None, "ka", None))

time: 54.2 us -> 52.7 us (0.972)
  local copies, waits for them, and re-layouts: 1.77 us -> 0.75 us
  Pallas kernels: 49.3 us -> 48.7 us
    unnamed x1, local copies, waits for them, and re-layouts: 1.77 us -> 0.75 us
    pallas_call x1, Pallas kernels: 49.3 us -> 48.7 us  [shards(): pl.pallas_call(functools.partial(chosen, groups, levels, rows, batches),...]
where the time goes in v7:
time: 52.7 us; the launch traced here: 51.8 us
  Pallas kernels  48.7 us (92%)
  between operations  2.33 us (4%)
  local copies, waits for them, and re-layouts  0.75 us (1%)
    pallas_call x1, Pallas kernels, shards(): pl.pallas_call(functools.partial(chosen, groups, levels, rows, batches),...  48.7 us

profile of v7, /device:TPU:0, one launch (start us, length us, event | category | flops | bytes accessed | tf_op | source)
XLA Modules:
  0.0 51.8 jit_solution(4736215434028745414)
XLA Ops:
  0.6 48.7 %shard_map.41 = (f32[2,384,128]{2,1,0:T(8,128)S(1)}, f32[1,1]{1,0:T(1,128)}) custom-call(f32[2,384,256]{2,1,0:T(8,128)} %t_hbm.1, f32[2,384,128]{2,1,0:T(8,128)} %s_hbm.1), custom_call_target="tpu_custom_call" | custom-call | tf_op jit(solution)/shard_map/pallas_call | solution.py:1197
  49.3 0.7 %copy.6 = f32[2,384,128]{2,1,0:T(8,128)} copy(f32[2,384,128]{2,1,0:T(8,128)S(1)} %get-tuple-element.8) | data formatting | bytes 786432

commit v8 on v7

--- a/solution.py
+++ b/solution.py
@@ -15,6 +15,8 @@
 LANES = 128
 TILE = 64
 PART = 32
+WIDE = 192
+STEP = 256
 MESH = pl.DeviceIdType.MESH
 LOG2E = 1.4426950408889634
 LN2 = 0.6931471805599453
@@ -506,14 +508,24 @@
     count = 2 * groups * levels
     index = place * levels + z
 
-    def greet(step, carry):
+    def greet(step, told):
         other = (index + step) % count
         spot, level = other // levels, other % levels
-        device = ((spot % groups) * batches + seq, level * 2 + spot // groups)
-        pl.semaphore_signal(barrier, inc=1, device_id=device, device_id_type=MESH)
-        return carry
-
-    lax.fori_loop(1, count, greet, 0)
+        inside = jnp.logical_and(level > 0, level < levels - 1)
+        meets = jnp.logical_or(
+            level == z,
+            jnp.logical_or(
+                jnp.logical_and(inside, inner_level), jnp.logical_and(spot % groups == y, outer)
+            ),
+        )
+
+        @pl.when(meets)
+        def _():
+            device = ((spot % groups) * batches + seq, level * 2 + spot // groups)
+            pl.semaphore_signal(barrier, inc=1, device_id=device, device_id_type=MESH)
+        return told + jnp.where(meets, 1, 0)
+
+    greeted = lax.fori_loop(1, count, greet, 0)
     diagonal = (1 - y) * batches + (1 - seq)
     for other in (mate, diagonal):
         pl.semaphore_signal(barrier, inc=1, device_id=(other, ka), device_id_type=MESH)
@@ -529,7 +541,7 @@
             pltpu.make_async_copy(s_hbm.at[seq], col_s.at[slot], slot_sem.at[slot, 1]).start()
     for load in loads:
         load.start()
-    pl.semaphore_wait(barrier, count + 1)
+    pl.semaphore_wait(barrier, greeted + 2)
 
     y_device = ((1 - y) * batches + seq, ka)
 
@@ -850,14 +862,14 @@
         for step in range(1, levels):
             div_copy(step, z).start()
 
-    tiles = 2 * rows // TILE
+    tiles = 2 * rows // WIDE
 
     def row_weights(xb):
         rows_t = wide[xb, 0:1, :]
         rows_s = wide[xb, 1:2, :]
 
         def tile(j, carry):
-            at = pl.ds(pl.multiple_of(j * TILE, TILE), TILE)
+            at = pl.ds(pl.multiple_of(j * WIDE, WIDE), WIDE)
             w_row[xb, at, :] = jnp.exp2(s_sc[xb, at, :] - rows_s) - jnp.exp2(t_sc[xb, at, :] - rows_t)
             return carry
 
@@ -926,8 +938,9 @@
         )
 
     def gradient(xb):
-        def tile(j, carry):
-            at = pl.ds(pl.multiple_of(j * TILE, TILE), TILE)
+        product = jnp.zeros((DS, rows), jnp.float32)
+        for start in range(0, 2 * rows, STEP):
+            at = slice(start, start + STEP)
             col = col_level[at, :]
             weight = (
                 w_row[xb, at, :]
@@ -937,11 +950,8 @@
             high_part, low_part = split(weight)
             w_high[at, :] = high_part
             w_low[at, :] = low_part
-            return carry
-
-        lax.fori_loop(0, tiles, tile, 0)
-        first = nn(q_tr[...], w_high[...])
-        product = first[:DS] + first[DS:] + nn(q_tr[0:DS, :], w_low[...])
+            first = nn(q_tr[:, at], high_part)
+            product = product + (first[:DS] + first[DS:] + nn(q_tr[0:DS, at], low_part))
         for b in range(blocks):
             part[xb, b] = product[:, b * LANES:(b + 1) * LANES]
 

time: 52.7 us -> 50.7 us (0.962)
  Pallas kernels: 48.7 us -> 46.7 us
    pallas_call x1, Pallas kernels: 48.7 us -> 46.7 us  [shards(): pl.pallas_call(functools.partial(chosen, groups, levels, rows, batches),...]
where the time goes in v8:
time: 50.7 us; the launch traced here: 49.8 us
  Pallas kernels  46.7 us (92%)
  between operations  2.33 us (5%)
  local copies, waits for them, and re-layouts  0.75 us (1%)
    pallas_call x1, Pallas kernels, shards(): pl.pallas_call(functools.partial(chosen, groups, levels, rows, batches),...  46.7 us

profile of v8, /device:TPU:0, one launch (start us, length us, event | category | flops | bytes accessed | tf_op | source)
XLA Modules:
  0.0 49.8 jit_solution(11003444782105209742)
XLA Ops:
  0.6 46.7 %shard_map.41 = (f32[2,384,128]{2,1,0:T(8,128)S(1)}, f32[1,1]{1,0:T(1,128)}) custom-call(f32[2,384,256]{2,1,0:T(8,128)} %t_hbm.1, f32[2,384,128]{2,1,0:T(8,128)} %s_hbm.1), custom_call_target="tpu_custom_call" | custom-call | tf_op jit(solution)/shard_map/pallas_call | solution.py:1207
  47.3 0.7 %copy.6 = f32[2,384,128]{2,1,0:T(8,128)} copy(f32[2,384,128]{2,1,0:T(8,128)S(1)} %get-tuple-element.8) | data formatting | bytes 786432

commit v9 on v8

--- a/solution.py
+++ b/solution.py
@@ -598,27 +598,25 @@
         s_high, s_low = split(col_s[:, span, :].reshape(2 * CHUNK, DS))
         teacher = nn(jnp.concatenate([t_high, t_high, t_low], axis=1), row_t[xb])
         student = nn(jnp.concatenate([s_high, s_high, s_low], axis=1), row_s[xb])
-        tiles = []
         for slot in range(2):
-            base = slot * rows + j * CHUNK
-            at = pl.ds(pl.multiple_of(base, CHUNK), CHUNK)
+            at = pl.ds(pl.multiple_of(slot * rows + j * CHUNK, PART), CHUNK)
             t_sc[xb, at, :] = teacher[slot * CHUNK:(slot + 1) * CHUNK]
             s_sc[xb, at, :] = student[slot * CHUNK:(slot + 1) * CHUNK]
-            tiles += [pl.ds(pl.multiple_of(base + i * PART, PART), PART) for i in range(CHUNK // PART)]
-
-        def read(ref, at):
-            return ref[xb, at, :].reshape(PART // 8, 8, rows)
+        tiles = range(0, 2 * CHUNK, PART)
+
+        def read(values, at):
+            return values[at:at + PART].reshape(PART // 8, 8, rows)
 
         t_old, s_old = acc[xb, 0], acc[xb, 3]
         t_max, s_max = t_old, s_old
         for at in tiles:
-            t_max = jnp.maximum(t_max, jnp.max(read(t_sc, at), axis=0))
-            s_max = jnp.maximum(s_max, jnp.max(read(s_sc, at), axis=0))
+            t_max = jnp.maximum(t_max, jnp.max(read(teacher, at), axis=0))
+            s_max = jnp.maximum(s_max, jnp.max(read(student, at), axis=0))
         t_scale = jnp.exp2(t_old - t_max)
         s_scale = jnp.exp2(s_old - s_max)
         t_sum, cross, s_sum = acc[xb, 1] * t_scale, acc[xb, 2] * t_scale, acc[xb, 4] * s_scale
         for at in tiles:
-            t_tile, s_tile = read(t_sc, at), read(s_sc, at)
+            t_tile, s_tile = read(teacher, at), read(student, at)
             t_exp = jnp.exp2(t_tile - t_max[None])
             t_sum = t_sum + jnp.sum(t_exp, axis=0)
             cross = cross + jnp.sum(t_exp * (t_tile - s_tile), axis=0)

time: 50.7 us -> 50.6 us (level)
  no operation moved by 1% of the time
where the time goes in v9:
time: 50.6 us; the launch traced here: 49.6 us
  Pallas kernels  46.6 us (92%)
  between operations  2.33 us (5%)
  local copies, waits for them, and re-layouts  0.75 us (1%)
    pallas_call x1, Pallas kernels, shards(): pl.pallas_call(functools.partial(chosen, groups, levels, rows, batches),...  46.6 us

profile of v9, /device:TPU:0, one launch (start us, length us, event | category | flops | bytes accessed | tf_op | source)
XLA Modules:
  0.0 49.6 jit_solution(3143760168530199416)
XLA Ops:
  0.6 46.6 %shard_map.41 = (f32[2,384,128]{2,1,0:T(8,128)S(1)}, f32[1,1]{1,0:T(1,128)}) custom-call(f32[2,384,256]{2,1,0:T(8,128)} %t_hbm.1, f32[2,384,128]{2,1,0:T(8,128)} %s_hbm.1), custom_call_target="tpu_custom_call" | custom-call | tf_op jit(solution)/shard_map/pallas_call | solution.py:1205
  47.2 0.7 %copy.6 = f32[2,384,128]{2,1,0:T(8,128)} copy(f32[2,384,128]{2,1,0:T(8,128)S(1)} %get-tuple-element.8) | data formatting | bytes 786432

commit v10 on v9

--- a/solution.py
+++ b/solution.py
@@ -915,12 +915,12 @@
             device_id=(((y + step) % groups) * batches + seq, ka), device_id_type=MESH,
         )
 
-    def out_copy(which, b):
+    def out_copy(which, b, to):
         span = pl.ds(b * LANES, LANES)
         return pltpu.make_async_remote_copy(
             src_ref=out_ref.at[which, span, :], dst_ref=out_ref.at[which, span, :],
-            send_sem=out_send.at[b], recv_sem=out_recv.at[b],
-            device_id=(mate, ka), device_id_type=MESH,
+            send_sem=out_send.at[to, b], recv_sem=out_recv.at[which, b],
+            device_id=totals[to], device_id_type=MESH,
         )
 
     totals = [(((1 - y) * batches + seq), ka), (mate, ka), (diagonal, ka)]
@@ -984,8 +984,6 @@
             for slot in range(2):
                 turned_copy(slot, b).start()
 
-    sends_y = jnp.logical_or(inner_level, outer)
-    gets_y = jnp.logical_or(inner_level, jnp.logical_not(outer))
     for b in range(blocks):
         @pl.when(active)
         def _():
@@ -998,7 +996,7 @@
                 landed(turned_in.at[level, b], pz_recv.at[level, b])
             x_sum[b] = x_sum[b] + (turned_in[0, b] + turned_in[1, b]).T
 
-        @pl.when(sends_y)
+        @pl.when(inner_level)
         def _():
             py_copy(1, b).start()
 
@@ -1016,22 +1014,17 @@
     for b in range(blocks):
         span = slice(b * LANES, (b + 1) * LANES)
 
-        @pl.when(gets_y)
+        @pl.when(inner_level)
         def _():
             py_copy(1, b).wait_recv()
-
-        @pl.when(inner_level)
-        def _():
             out_ref[seq, span, :] = (x_sum[b] + y_in[1, b]).T
+            out_copy(seq, b, 1).start()
 
         @pl.when(outer_end)
         def _():
             out_ref[seq, span, :] = x_sum[b].T
-
-        @pl.when(jnp.logical_not(active))
-        def _():
-            out_ref[seq, span, :] = y_in[1, b].T
-        out_copy(seq, b).start()
+            for to in range(3):
+                out_copy(seq, b, to).start()
 
     landed(total_in.at[1 - seq], total_recv.at[1 - seq])
 
@@ -1093,11 +1086,23 @@
             for slot in range(2):
                 turned_copy(slot, b).wait_send()
 
-        @pl.when(sends_y)
+        @pl.when(inner_level)
         def _():
             py_copy(1, b).wait_send()
-        out_copy(seq, b).wait_send()
-        out_copy(1 - seq, b).wait_recv()
+
+        @pl.when(active)
+        def _():
+            out_copy(seq, b, 1).wait_send()
+
+        @pl.when(outer_end)
+        def _():
+            out_copy(seq, b, 0).wait_send()
+            out_copy(seq, b, 2).wait_send()
+
+        @pl.when(jnp.logical_not(active))
+        def _():
+            out_copy(seq, b, 1).wait_recv()
+        out_copy(1 - seq, b, 1).wait_recv()
 
 
 def solution(mesh):
@@ -1162,8 +1167,8 @@
             dma((groups, blocks)),
             dma((2, blocks)),
             dma((2, blocks)),
-            dma((blocks,)),
-            dma((blocks,)),
+            dma((3, blocks)),
+            dma((2, blocks)),
             dma((3,)),
             dma((2,)),
         ] if folds else [

time: 50.6 us -> 53.1 us (1.049); the launches traced: 49.6 us -> 52.9 us
  Pallas kernels: 46.6 us -> 49.8 us
    pallas_call x1, Pallas kernels: 46.6 us -> 49.8 us  [shards(): pl.pallas_call(functools.partial(chosen, groups, levels, rows, batches),...]
where the time goes in v10:
time: 53.1 us; the launch traced here: 52.9 us
  Pallas kernels  49.8 us (94%)
  between operations  2.33 us (4%)
  local copies, waits for them, and re-layouts  0.75 us (1%)
    pallas_call x1, Pallas kernels, shards(): pl.pallas_call(functools.partial(chosen, groups, levels, rows, batches),...  49.8 us

profile of v10, /device:TPU:0, one launch (start us, length us, event | category | flops | bytes accessed | tf_op | source)
XLA Modules:
  0.0 52.9 jit_solution(16612234830334398409)
XLA Ops:
  0.6 49.8 %shard_map.41 = (f32[2,384,128]{2,1,0:T(8,128)S(1)}, f32[1,1]{1,0:T(1,128)}) custom-call(f32[2,384,256]{2,1,0:T(8,128)} %t_hbm.1, f32[2,384,128]{2,1,0:T(8,128)} %s_hbm.1), custom_call_target="tpu_custom_call" | custom-call | tf_op jit(solution)/shard_map/pallas_call | solution.py:1210
  50.5 0.7 %copy.6 = f32[2,384,128]{2,1,0:T(8,128)} copy(f32[2,384,128]{2,1,0:T(8,128)S(1)} %get-tuple-element.8) | data formatting | bytes 786432
